TPU v7x, 32 devices: a whole 2x2x4 slice. The times are simulated.
32 devices in a mesh: line: 4 (over y, x), tile: 8 (over z, core).
Axes of the slice: x: 2, y: 2, z: 4, core: 2. Of those that a mesh axis runs over, the one named last changes fastest.
Arguments:
- forcing: float32 [10, 64, 8, 512], P(None, None, 'tile', 'line'), may hold values from -1100 to 1100
- block_inverse: float32 [10, 10, 8, 512], P(None, None, 'tile', 'line'), may hold values from -0.8 to 1
- wall_rates: float32 [2, 10, 8, 512], P(None, None, 'tile', 'line'), may hold values from 0 to 1, as said below
- span_couple: float32 [10], replicated, may hold values from 0.1 to 0.4
Outputs:
- basis: float32 [10, 64, 8, 512], P(None, None, 'tile', 'line')
Inputs may be any that keep to these rules, and one draw needn't show every extreme that they name: `wall_rates`: every entry lies strictly between 0 and 1.
All inputs are finite; a program needn't handle non-finite values.
Results may differ from a plain program's by a relative error of at most 0.00022.
Values sent between devices are 32-bit elements; how exact they have to be, the bound alone decides.
A program may use at most 64 MiB of HBM per device.

v0:
```python
import math

import jax
import jax.numpy as jnp
from jax import lax
from jax.sharding import PartitionSpec as P


def prefix(value, axis, combine, identity, reverse):
    peers, mine = (lax.axis_size(axis), lax.axis_index(axis))
    everything = jax.tree.map(lambda part: lax.all_gather(part, axis), value)
    start = jax.tree.map(
        lambda part, zero: jnp.broadcast_to(jnp.asarray(zero, part.dtype), part.shape),
        value,
        identity,
    )

    def step(k, before):
        at = peers - 1 - k if reverse else k
        reached = at > mine if reverse else at < mine
        new = combine(before, jax.tree.map(lambda part: part[at], everything))
        return jax.tree.map(lambda a, b: jnp.where(reached, a, b), new, before)

    return lax.fori_loop(0, peers, step, start)


def with_halo(block, sides, width):
    for axis, dim in sides:
        count = lax.axis_size(axis)
        forward = [(i, i + 1) for i in range(count - 1)]
        forward.append((count - 1, 0))
        backward = [(target, source) for source, target in forward]
        low = lax.ppermute(
            lax.slice_in_dim(block, block.shape[dim] - width, None, axis=dim), axis, forward
        )
        high = lax.ppermute(lax.slice_in_dim(block, 0, width, axis=dim), axis, backward)
        block = jnp.concatenate([low, block, high], axis=dim)
    return block


def from_behind(value, axis, by):
    peers = lax.axis_size(axis)
    pairs = [(i, i + by) for i in range(peers) if 0 <= i + by < peers]
    return lax.ppermute(value, axis, pairs)


def apply_block(blocks, values_in):
    n_comp = blocks.shape[0]
    running = blocks[:, 0][:, None] * values_in[0][None]
    for member in range(1, n_comp):
        running = running + blocks[:, member][:, None] * values_in[member][None]
    return running


def compose(earlier, later):
    return (earlier[0] * later[0], later[0] * earlier[1] + later[1])


def local_scan(survival_fraction, source, backward):
    return lax.associative_scan(compose, (survival_fraction, source), reverse=backward, axis=3)


def chain_entry(end_rate, end_value, backward):
    identity_pair = (jnp.ones_like(end_rate), jnp.zeros_like(end_value))
    if backward:
        result = prefix((end_rate, end_value), "line", compose, identity_pair, True)
    else:
        result = prefix((end_rate, end_value), "line", compose, identity_pair, False)
    entry_value = result[1]
    return entry_value


def local(forcing, block_inverse, wall_rates, span_couple):
    n_comp, n_cols, n_station, n_point = forcing.shape
    row_count = n_comp * n_station * lax.axis_size("tile") * n_point * lax.axis_size("line")
    coupling = span_couple[:, None, None, None]
    rise_rate = wall_rates[0][:, None]
    fall_rate = wall_rates[1][:, None]
    start_field = apply_block(block_inverse, forcing)
    padded_start = with_halo(start_field, (("tile", 2),), 1)
    beside_zero = padded_start[:, :, :-2] + padded_start[:, :, 2:]
    next_row = from_behind(start_field[..., 0], "line", -1)
    above_row = jnp.concatenate([start_field[..., 1:], next_row[..., None]], axis=-1)
    source_one = (
        apply_block(block_inverse, forcing + coupling * beside_zero) + fall_rate * above_row
    )
    product_one, local_one = local_scan(rise_rate, source_one, False)
    entry_one = chain_entry(product_one[..., -1], local_one[..., -1], False)
    rising = product_one * entry_one[..., None] + local_one
    local_pad = with_halo(local_one, (("tile", 2),), 1)
    product_pad = with_halo(product_one, (("tile", 2),), 1)
    entry_pad = with_halo(entry_one, (("tile", 2),), 1)
    rim_low = product_pad[:, :, :1] * entry_pad[:, :, :1, None] + local_pad[:, :, :1]
    rim_high = product_pad[:, :, -1:] * entry_pad[:, :, -1:, None] + local_pad[:, :, -1:]
    padded_one = jnp.concatenate([rim_low, rising, rim_high], axis=2)
    beside_one = padded_one[:, :, :-2] + padded_one[:, :, 2:]
    below_row = jnp.concatenate([entry_one[..., None], rising[..., :-1]], axis=-1)
    source_two = apply_block(block_inverse, forcing + coupling * beside_one) + rise_rate * below_row
    product_two, local_two = local_scan(fall_rate, source_two, True)
    entry_two = chain_entry(product_two[..., 0], local_two[..., 0], True)
    falling = product_two * entry_two[..., None] + local_two
    local_gram = jnp.einsum("krzj,kszj->rs", falling, falling, precision=lax.Precision.HIGHEST)
    gram = lax.psum(local_gram, ("line", "tile"))
    lower_factor = jnp.linalg.cholesky(gram)
    identity_matrix = jnp.eye(n_cols, dtype=gram.dtype)
    inverse_factor = jax.scipy.linalg.solve_triangular(lower_factor, identity_matrix, lower=True).T
    scale_value = math.sqrt(row_count)
    return (
        jnp.einsum("krzj,rs->kszj", falling, inverse_factor, precision=lax.Precision.HIGHEST)
        * scale_value
    )


def solution(mesh):
    in_specs = (
        P(None, None, "tile", "line"),
        P(None, None, "tile", "line"),
        P(None, None, "tile", "line"),
        P(),
    )
    out_specs = P(None, None, "tile", "line")
    return jax.shard_map(local, mesh=mesh, in_specs=in_specs, out_specs=out_specs, check_vma=False)
```

profile of v0, /device:TPU:0, one launch (start us, length us, event | category | flops | bytes accessed | tf_op | source)
XLA Modules:
  0.0 132.1 jit_solution(4113493527768575870)
XLA Ops:
  0.0 0.7 fusion.30
  1.9 0.6 slice-done.2
  2.9 4.5 %collective-permute-start.6 = (f32[10,1,1,128]{0,3,2,1:T(8,128)S(1)}, f32[10,1,1,128]{0,3,2,1:T(8,128)S(1)}, u32[]{:S(2)}, u32[]{:S(2)}) collective-permute-start(f32[10,1,1,128]{0,3,2,1:T(8,128)S(1)} %add.714), channel_id=1, source_target_pairs={{1,0},{2,1},{3,2},{4,3},{5,4},{6,5},{7,6},{0,7},{9,8},{10,9},{11,1... | collective-permute-start | bytes 15368 | tf_op jit(solution)/shard_map/ppermute | solution.py:36
  8.6 1.8 %multiply_add_fusion.1 = f32[10,64,1,128]{1,3,2,0:T(8,128)S(1)} fusion(f32[64,128]{0,1:T(8,128)S(1)} %copy.544, f32[10,128]{1,0:T(8,128)S(1)} %get-tuple-element.443, f32[64,128]{0,1:T(8,128)S(1)} %copy.543, f32[10,128]{1,0:T(8,128)S(1)} %get-tuple-element.444, f32[64,128]{0,1:T(8,128)S(1)} %copy.542, f32[10,128]{1,0:T(8,128)S(1)} %get-tuple-element.445, ...), kind=kLoop, calls=%fused_computation.19 | loop fusion | flops 1556480 | bytes 706560 | tf_op jit(solution)/shard_map/add | solution.py:51
  10.6 3.6 %collective-permute-start.2 = (f32[10,64,1,128]{3,1,2,0:T(8,128)S(1)}, f32[10,64,1,128]{3,1,2,0:T(8,128)S(1)}, u32[]{:S(2)}, u32[]{:S(2)}) collective-permute-start(f32[10,64,1,128]{3,1,2,0:T(8,128)S(1)} %copy.545), channel_id=1, source_target_pairs={{1,0},{2,1},{3,2},{4,3},{5,4},{6,5},{7,6},{0,7},{9,8},{10,9},{11,1... | collective-permute-start | bytes 983048 | tf_op jit(solution)/shard_map/ppermute | solution.py:36
  14.2 1.3 collective-permute-start.3
  16.8 0.6 slice-done.3
  17.7 0.6 copy-done.7
  21.9 11.1 %all-reduce.58 = (f32[40]{0:T(128)S(1)}, f32[40]{0:T(128)S(1)}) all-reduce(f32[40]{0:T(128)S(1)} %fusion.23, f32[40]{0:T(128)S(1)} %fusion.24), channel_id=3, replica_groups=mesh['line'=4,'tile'=8] {'line'}, use_global_device_ids=true, to_apply=%add.57 | all-reduce | flops 80 | bytes 640
  33.4 0.6 copy-done.6
  35.2 2.1 %fusion = f32[10,64,1,128]{1,3,2,0:T(8,128)S(1)} fusion(f32[10,64,1,1]{1,3,2,0:T(1,128)S(1)} %bitcast.250, f32[10,64,1,127]{1,3,2,0:T(8,128)S(1)} %slice.818, f32[10,128]{1,0:T(8,128)S(1)} %bitcast.240, f32[64,128]{0,1:T(8,128)S(1)} %copy.557, f32[64,128]{0,1:T(8,128)S(1)} %copy.556, f32[64,128]{0,1:T(8,128)S(1)} %copy.555, f32[64,128]{0,1:T(8,128)S(1)} %copy.554, ...), kind=kLoop, calls=%fused_computation.13 | loop fusion | flops 1802240 | bytes 1039360 | tf_op jit(solution)/shard_map/add | solution.py:85
  45.1 1.3 collective-permute-start.8
  46.4 7.2 %all-gather.2 = f32[40,64,1,1]{1,3,2,0:T(1,128)S(1)} all-gather(f32[10,64,1,1]{1,3,2,0:T(1,128)S(1)} %slice_add_fusion.3), channel_id=4, replica_groups=mesh['line'=4,'tile'=8] {'line'}, dimensions={0}, use_global_device_ids=true | all-gather | bytes 12800 | tf_op jit(solution)/shard_map/all_gather | solution.py:11
  54.2 3.5 %collective-permute-start.7 = (f32[10,64,1]{1,2,0:T(1,128)S(1)}, f32[10,64,1]{1,2,0:T(1,128)S(1)}, u32[]{:S(2)}, u32[]{:S(2)}) collective-permute-start(f32[10,64,1]{1,2,0:T(1,128)S(1)} %get-tuple-element.231), channel_id=1, source_target_pairs={{1,0},{2,1},{3,2},{4,3},{5,4},{6,5},{7,6},{0,7},{9,8},{10,9},{11,1... | collective-permute-start | bytes 7688 | tf_op jit(solution)/shard_map/ppermute | solution.py:36
  58.0 1.1 collective-permute-done.4
  60.3 2.1 %fusion.1 = f32[10,64,1,128]{1,3,2,0:T(8,128)S(1)} fusion(f32[10,64,1,127]{1,3,2,0:T(8,128)S(1)} %add_add_fusion, f32[10,64,1,1]{1,3,2,0:T(1,128)S(1)} %bitcast.210, f32[10,128]{1,0:T(8,128)S(1)} %bitcast.239, f32[64,128]{0,1:T(8,128)S(1)} %copy.585, f32[64,128]{0,1:T(8,128)S(1)} %copy.584, f32[64,128]{0,1:T(8,128)S(1)} %copy.583, f32[64,128]{0,1:T(8,128)S(1)} %copy.582, ...), kind=kLoop, calls=%fused_computation.15 | loop fusion | flops 1802240 | bytes 1039360 | tf_op jit(solution)/shard_map/add | solution.py:98
  70.5 8.3 %all-gather.3 = f32[40,64,1,1]{1,3,2,0:T(1,128)S(1)} all-gather(f32[10,64,1,1]{1,3,2,0:T(1,128)S(1)} %slice_add_fusion), channel_id=5, replica_groups=mesh['line'=4,'tile'=8] {'line'}, dimensions={0}, use_global_device_ids=true | all-gather | bytes 12800 | tf_op jit(solution)/shard_map/all_gather | solution.py:11
  79.4 1.6 %convolution_bitcast_fusion.1 = f32[64,64]{0,1:T(8,128)S(1)} fusion(f32[10,64,1,128]{1,3,2,0:T(8,128)S(1)} %rev.9, f32[10,64]{1,0:T(8,128)S(1)} %bitcast.227, f32[10,128]{1,0:T(8,128)S(1)} %copy.532), kind=kOutput, calls=%fused_computation.10 | convolution fusion | flops 63078400 | bytes 351744 | tf_op jit(solution)/shard_map/krzj,kszj->rs/dot_general | solution.py:102
  81.0 37.0 %psum.7 = f32[64,64]{0,1:T(8,128)S(1)} all-reduce(f32[64,64]{0,1:T(8,128)S(1)} %convolution_bitcast_fusion.1), channel_id=1, replica_groups=mesh['line'=4,'tile'=8] {'line','tile'}, use_global_device_ids=true, to_apply=%region_4.5 | all-reduce | flops 4096 | bytes 32768 | tf_op jit(solution)/shard_map/psum | solution.py:103
  118.1 5.8 %cholesky.17 = f32[64,64]{1,0:T(8,128)S(1)} custom-call(f32[64,64]{1,0:T(8,128)S(1)} %fusion.18), custom_call_target="Cholesky" | custom-call | tf_op jit(solution)/shard_map/jit(cholesky)/cholesky | solution.py:104
  124.0 0.6 compare_reduce_fusion
  124.7 0.7 fusion.16
  125.3 4.9 %custom-call.7 = f32[1,64,64]{1,2,0:T(8,128)S(1)} custom-call(f32[1,64,64]{2,1,0:T(8,128)S(1)} %fusion.16), custom_call_target="InvertDiagBlocksLowerTriangular" | custom-call | tf_op jit(solution)/shard_map/jit(_solve_triangular)/triangular_solve | solution.py:106
  130.5 1.6 %convolution_multiply_fusion = f32[64,10,128]{2,0,1:T(8,128)} fusion(f32[64,64,1]{1,0,2:T(8,128)S(1)} %convolution_bitcast_fusion, f32[10,64,1,128]{1,3,2,0:T(8,128)S(1)} %rev.9, f32[10,64]{1,0:T(8,128)S(1)} %bitcast.228, f32[10,128]{1,0:T(8,128)S(1)} %copy.532), kind=kOutput, calls=%fused_computation.8 | convolution fusion | flops 63160320 | bytes 679424 | tf_op jit(solution)/shard_map/krzj,rs->kszj/dot_general | solution.py:109
  (389 shorter events, 27.0 us)
Async XLA Ops:
  1.1 0.6 copy-start.4
  1.9 0.7 slice-start.2
  2.8 4.7 %copy-start = (f32[10,64,1,128]{3,2,1,0:T(1,128)S(1)}, f32[10,64,1,128]{3,2,1,0:T(1,128)}, u32[]{:S(2)}) copy-start(f32[10,64,1,128]{3,2,1,0:T(1,128)} %param.8) | copy-start | bytes 983044
  2.9 4.6 %copy-start.3 = (f32[10,10,1,128]{3,2,1,0:T(1,128)S(1)}, f32[10,10,1,128]{3,2,1,0:T(1,128)}, u32[]{:S(2)}) copy-start(f32[10,10,1,128]{3,2,1,0:T(1,128)} %param.9) | copy-start | bytes 153604
  2.9 30.3 %collective-permute-start.6 = (f32[10,1,1,128]{0,3,2,1:T(8,128)S(1)}, f32[10,1,1,128]{0,3,2,1:T(8,128)S(1)}, u32[]{:S(2)}, u32[]{:S(2)}) collective-permute-start(f32[10,1,1,128]{0,3,2,1:T(8,128)S(1)} %add.714), channel_id=1, source_target_pairs={{1,0},{2,1},{3,2},{4,3},{5,4},{6,5},{7,6},{0,7},{9,8},{10,9},{11,1... | collective-permute-start | bytes 15368 | tf_op jit(solution)/shard_map/ppermute | solution.py:36
  7.4 25.9 %collective-permute-start = (f32[10,1,1,128]{0,3,2,1:T(8,128)S(1)}, f32[10,1,1,128]{0,3,2,1:T(8,128)S(1)}, u32[]{:S(2)}, u32[]{:S(2)}) collective-permute-start(f32[10,1,1,128]{0,3,2,1:T(8,128)S(1)} %add.714), channel_id=1, source_target_pairs={{0,1},{1,2},{2,3},{3,4},{4,5},{5,6},{6,7},{7,0},{8,9},{9,10},{10,1... | collective-permute-start | bytes 15368 | tf_op jit(solution)/shard_map/ppermute | solution.py:33
  10.6 22.8 %collective-permute-start.2 = (f32[10,64,1,128]{3,1,2,0:T(8,128)S(1)}, f32[10,64,1,128]{3,1,2,0:T(8,128)S(1)}, u32[]{:S(2)}, u32[]{:S(2)}) collective-permute-start(f32[10,64,1,128]{3,1,2,0:T(8,128)S(1)} %copy.545), channel_id=1, source_target_pairs={{1,0},{2,1},{3,2},{4,3},{5,4},{6,5},{7,6},{0,7},{9,8},{10,9},{11,1... | collective-permute-start | bytes 983048 | tf_op jit(solution)/shard_map/ppermute | solution.py:36
  14.2 19.2 %collective-permute-start.1 = (f32[10,64,1,128]{3,1,2,0:T(8,128)S(1)}, f32[10,64,1,128]{3,1,2,0:T(8,128)S(1)}, u32[]{:S(2)}, u32[]{:S(2)}) collective-permute-start(f32[10,64,1,128]{3,1,2,0:T(8,128)S(1)} %copy.545), channel_id=1, source_target_pairs={{0,1},{1,2},{2,3},{3,4},{4,5},{5,6},{6,7},{7,0},{8,9},{9,10},{10,1... | collective-permute-start | bytes 983048 | tf_op jit(solution)/shard_map/ppermute | solution.py:33
  14.2 21.0 %collective-permute-start.3 = (f32[10,64,1]{1,2,0:T(1,128)S(1)}, f32[10,64,1]{1,2,0:T(1,128)S(1)}, u32[]{:S(2)}, u32[]{:S(2)}) collective-permute-start(f32[10,64,1]{1,2,0:T(1,128)S(1)} %slice_bitcast_fusion.20), channel_id=1, source_target_pairs={{8,0},{16,8},{24,16},{9,1},{17,9},{25,17},{10,2},{18,10},{26,18},{... | collective-permute-start | bytes 7688 | tf_op jit(solution)/shard_map/ppermute | solution.py:44
  15.9 0.6 copy-start.5
  16.7 0.7 slice-start.3
  17.6 0.7 copy-start.7
  33.4 0.7 copy-start.6
  40.5 0.6 copy-start.1
  42.4 0.7 slice-start
  45.1 13.9 %collective-permute-start.8 = (f32[10,64,1,128]{3,1,2,0:T(8,128)S(1)}, f32[10,64,1,128]{3,1,2,0:T(8,128)S(1)}, u32[]{:S(2)}, u32[]{:S(2)}) collective-permute-start(f32[10,64,1,128]{3,1,2,0:T(8,128)S(1)} %copy.572), channel_id=1, source_target_pairs={{1,0},{2,1},{3,2},{4,3},{5,4},{6,5},{7,6},{0,7},{9,8},{10,9},{11,1... | collective-permute-start | bytes 983048 | tf_op jit(solution)/shard_map/ppermute | solution.py:36
  46.4 12.7 %collective-permute-start.5 = (f32[10,64,1,128]{3,1,2,0:T(8,128)S(1)}, f32[10,64,1,128]{3,1,2,0:T(8,128)S(1)}, u32[]{:S(2)}, u32[]{:S(2)}) collective-permute-start(f32[10,64,1,128]{3,1,2,0:T(8,128)S(1)} %copy.572), channel_id=1, source_target_pairs={{0,1},{1,2},{2,3},{3,4},{4,5},{5,6},{6,7},{7,0},{8,9},{9,10},{10,1... | collective-permute-start | bytes 983048 | tf_op jit(solution)/shard_map/ppermute | solution.py:33
  54.1 4.9 %collective-permute-start.4 = (f32[10,64,1]{1,2,0:T(1,128)S(1)}, f32[10,64,1]{1,2,0:T(1,128)S(1)}, u32[]{:S(2)}, u32[]{:S(2)}) collective-permute-start(f32[10,64,1]{1,2,0:T(1,128)S(1)} %get-tuple-element.231), channel_id=1, source_target_pairs={{0,1},{1,2},{2,3},{3,4},{4,5},{5,6},{6,7},{7,0},{8,9},{9,10},{10,1... | collective-permute-start | bytes 7688 | tf_op jit(solution)/shard_map/ppermute | solution.py:33
  54.2 4.9 %collective-permute-start.7 = (f32[10,64,1]{1,2,0:T(1,128)S(1)}, f32[10,64,1]{1,2,0:T(1,128)S(1)}, u32[]{:S(2)}, u32[]{:S(2)}) collective-permute-start(f32[10,64,1]{1,2,0:T(1,128)S(1)} %get-tuple-element.231), channel_id=1, source_target_pairs={{1,0},{2,1},{3,2},{4,3},{5,4},{6,5},{7,6},{0,7},{9,8},{10,9},{11,1... | collective-permute-start | bytes 7688 | tf_op jit(solution)/shard_map/ppermute | solution.py:36
  65.8 0.6 copy-start.2
  67.8 0.7 slice-start.1
where the time goes:
time: 133 us; the launch traced here: 132 us
  blocking collectives  63.6 us (48%)
  local copies, waits for them, and re-layouts  23.8 us (18%)
  other arithmetic  23.1 us (17%)
  starting transfers between devices  14.3 us (11%)
  matrix products  3.47 us (3%)
  between operations  2.5 us (2%)
    psum x1, blocking collectives, local(): gram = lax.psum(local_gram, ('line', 'tile'))  37 us
    all_gather x2, blocking collectives, prefix(): everything = jax.tree.map(lambda part: lax.all_gather(part, axis), value)  15.6 us
    ppermute x4, starting transfers between devices, with_halo(): lax.ppermute(lax.slice_in_dim(block, 0, width, axis=dim), axis, backward)  12.9 us
    unnamed x1, blocking collectives  11.1 us
    slice x98, local copies, waits for them, and re-layouts, local_scan(): lax.associative_scan(compose, (survival_fraction, source), reverse=backwa...  10.8 us
    another operation x3, other arithmetic, local(): lower_factor = jnp.linalg.cholesky(gram)  6.52 us
    another operation x2, other arithmetic, local(): jax.scipy.linalg.solve_triangular(lower_factor, identity_matrix, lower=True)  5.55 us
    unnamed x31, local copies, waits for them, and re-layouts  3.53 us
  transfers between devices with their start and end apart: 9, of which 1 were waited for; matrix products, arithmetic and copies ran while one was open for 7% of the time, Pallas kernels for 0%

commit v1 on v0

v1 whole, which is shorter than its diff:
```python
import functools
import math

import jax
import jax.numpy as jnp
from jax import lax
from jax.experimental import pallas as pl
from jax.experimental.pallas import tpu as pltpu
from jax.sharding import PartitionSpec as P

MESH = pl.DeviceIdType.MESH
ROWS = 8


def reduce_phases(n_line, n_tile):
    pair = 2 if n_tile % 2 == 0 else 1
    phases = [(1, pair, True)]
    stride, rest = pair, n_tile // pair
    while rest > 1:
        factor = 4 if rest % 4 == 0 else next(f for f in range(2, rest + 1) if rest % f == 0)
        phases.append((stride, factor, False))
        stride, rest = stride * factor, rest // factor
    return phases


def phase_peers(phase, n_line):
    stride, factor, with_line = phase
    lines = n_line if with_line else 1
    return [(a, b) for a in range(lines) for b in range(factor) if (a, b) != (0, 0)]


def peer_id(phase, step, n_line):
    stride, factor, _ = phase
    line, tile = lax.axis_index("line"), lax.axis_index("tile")
    digit = lax.rem(lax.div(tile, stride), factor)
    there = lax.rem(digit + step[1], factor)
    return (lax.rem(line + step[0], n_line), tile + (there - digit) * stride)


def split(value):
    high = value.astype(jnp.bfloat16)
    low = (value - high.astype(jnp.float32)).astype(jnp.bfloat16)
    return high, low


def eliminate(gram):
    n = gram.shape[0]
    row = lax.broadcasted_iota(jnp.int32, (n, n), 0)
    col = lax.broadcasted_iota(jnp.int32, (n, n), 1)
    both = jnp.concatenate([gram, (row == col).astype(jnp.float32)], axis=1)
    blocks = [both[v * ROWS : (v + 1) * ROWS] for v in range(n // ROWS)]
    shape = (ROWS, 2 * n)
    sub = lax.broadcasted_iota(jnp.int32, shape, 0)
    scales = []
    for q in range(n // ROWS):
        live = range(q, n // ROWS)
        cols = [
            {v: jnp.broadcast_to(blocks[v][:, ROWS * q + c : ROWS * q + c + 1], shape) for v in live}
            for c in range(ROWS)
        ]
        scale = jnp.zeros(shape, jnp.float32)
        for c in range(ROWS):
            pivot = jnp.broadcast_to(cols[c][q][c : c + 1], shape)
            inv = 1.0 / pivot
            scale = jnp.where(sub == c, lax.rsqrt(pivot), scale)
            factor = {v: cols[c][v] * inv for v in live}
            factor[q] = jnp.where(sub > c, factor[q], 0.0)
            top = jnp.broadcast_to(blocks[q][c : c + 1], shape)
            tops = [jnp.broadcast_to(cols[e][q][c : c + 1], shape) for e in range(c + 1, ROWS)]
            for v in live:
                blocks[v] = blocks[v] - factor[v] * top
                for e in range(c + 1, ROWS):
                    cols[e][v] = cols[e][v] - factor[v] * tops[e - c - 1]
        scales.append(scale)
    return jnp.concatenate([b * s for b, s in zip(blocks, scales)], axis=0)[:, n:]


def kernel(
    n_line, n_tile, n_chunk, phases, scale_value,
    f_ref, a_ref, w_ref, s_ref, o_ref,
    start, z_low, z_high, rise, y_low, y_high, fall,
    edge_out, edge_in, ends_out, ends_in, enter, rates_out, rates_in, steps, whole,
    gram_out, gram_in, halo_send, halo_recv, edge_send, edge_recv, ends_send, ends_recv,
    rates_send, rates_recv, gram_send, gram_recv,
):
    n_comp, n_cols, n_point = f_ref.shape
    wide = n_cols // n_chunk
    line, tile = lax.axis_index("line"), lax.axis_index("tile")
    above, below = lax.rem(tile + 1, n_tile), lax.rem(tile + n_tile - 1, n_tile)
    line_peers = [(lax.rem(line + d, n_line), tile) for d in range(1, n_line)]
    lower_line = (lax.rem(line + n_line - 1, n_line), tile)
    gram_peers = [[peer_id(ph, step, n_line) for step in phase_peers(ph, n_line)] for ph in phases]

    greet = [(line, above), (line, below)] + [p for peers in gram_peers for p in peers]
    barrier = pltpu.get_barrier_semaphore()
    for peer in greet:
        pl.semaphore_signal(barrier, inc=1, device_id=peer, device_id_type=MESH)

    started = []

    def send(src, dst, send_sem, recv_sem, peer):
        copy = pltpu.make_async_remote_copy(
            src_ref=src, dst_ref=dst, send_sem=send_sem, recv_sem=recv_sem,
            device_id=peer, device_id_type=MESH,
        )
        copy.start()
        started.append(copy)
        return copy

    def cut(c):
        return pl.ds(c * wide, wide)

    lane3 = lax.broadcasted_iota(jnp.int32, (n_comp, 1, n_point), 2)
    lane = lax.broadcasted_iota(jnp.int32, (wide, n_point), 1)
    lane8 = lax.broadcasted_iota(jnp.int32, (ROWS, n_point), 1)
    lane_big = lax.broadcasted_iota(jnp.int32, (n_comp, wide, n_point), 2)
    n_steps = (n_point - 1).bit_length()

    def turn(value, by):
        flat = value.reshape(-1, n_point)
        return pltpu.roll(flat, by % n_point, 1).reshape(value.shape)

    def apply_block(value):
        total = a_ref[:, 0] * value[0][None]
        for m in range(1, n_comp):
            total = total + a_ref[:, m] * value[m][None]
        return total

    def pack(value, at):
        packed = jnp.zeros((value.shape[1], n_point), jnp.float32)
        places = lax.broadcasted_iota(jnp.int32, packed.shape, 1)
        for k in range(n_comp):
            packed = jnp.where(places == k, value[k][:, at : at + 1], packed)
        return packed

    def spread(packed):
        return jnp.stack(
            [jnp.broadcast_to(packed[:, k : k + 1], (wide, n_point)) for k in range(n_comp)], axis=0
        )

    def sweep(value, side):
        for i in range(n_steps):
            by = 1 << i
            value = value + steps[side, i] * turn(value, -by if side else by)
        return value

    halos = {}
    edges, ends, rates = [], {}, []

    def send_halo(which, c, field, low, high):
        halos[which, c] = [
            send(field.at[:, cut(c)], low.at[:, cut(c)], halo_send.at[which, c, 0],
                 halo_recv.at[which, c, 0], (line, above)),
            send(field.at[:, cut(c)], high.at[:, cut(c)], halo_send.at[which, c, 1],
                 halo_recv.at[which, c, 1], (line, below)),
        ]

    def send_ends(which, c):
        ends[which, c] = [
            send(ends_out.at[which, cut(c)], ends_in.at[which, d, cut(c)], ends_send.at[which, c, d],
                 ends_recv.at[which, c, d], peer)
            for d, peer in enumerate(line_peers)
        ]

    for c in range(n_chunk):
        field = apply_block(f_ref[:, c * wide : (c + 1) * wide])
        start[:, cut(c)] = field
        edge_out[cut(c)] = pack(field, 0)
        if c == 0:
            pl.semaphore_wait(barrier, len(greet))
        send_halo(0, c, start, z_low, z_high)
        edges.append(
            send(edge_out.at[cut(c)], edge_in.at[cut(c)], edge_send.at[c], edge_recv.at[c], lower_line)
        )

    for side in range(2):
        rate = w_ref[side]
        for i in range(n_steps):
            by = 1 << i
            inside = lane3 < n_point - by if side else lane3 >= by
            steps[side, i] = jnp.where(inside, rate, 0.0)
            rate = rate * jnp.where(inside, turn(rate, -by if side else by), 1.0)
        whole[side] = rate
        at = 0 if side else n_point - 1
        total = jnp.zeros((ROWS, n_point), jnp.float32)
        for k in range(n_comp):
            total = jnp.where(lane8 == k, rate[k][:, at : at + 1], total)
        rates_out[side] = total
    for d, peer in enumerate(line_peers):
        rates.append(send(rates_out, rates_in.at[d], rates_send.at[d], rates_recv.at[d], peer))

    def coupled(c, low, high):
        beside = low[:, c * wide : (c + 1) * wide] + high[:, c * wide : (c + 1) * wide]
        return jnp.stack(
            [f_ref[k, c * wide : (c + 1) * wide] + s_ref[k] * beside[k] for k in range(n_comp)], axis=0
        )

    def entry(which, c):
        for copy in ends[which, c]:
            copy.wait_recv()
        total = jnp.zeros((wide, n_point), jnp.float32)
        carried = jnp.ones((1, n_point), jnp.float32)
        for d in range(1, n_line):
            slot = n_line - d - 1 if which else d - 1
            reached = (line + d < n_line) if which else (line >= d)
            reached = reached.astype(jnp.float32)
            total = total + (carried * reached) * ends_in[which, slot, cut(c)]
            carried = carried * rates_in[slot, which, 0:1]
        return total

    def first(c):
        for copy in halos[0, c] + [edges[c]]:
            copy.wait_recv()
        source = apply_block(coupled(c, z_low, z_high))
        last = (line < n_line - 1).astype(jnp.float32)
        over = jnp.where(
            lane_big == n_point - 1, spread(edge_in[cut(c)] * last),
            turn(start[:, c * wide : (c + 1) * wide], -1),
        )
        value = sweep(source + w_ref[1] * over, 0)
        rise[:, cut(c)] = value
        ends_out[0, cut(c)] = pack(value, n_point - 1)
        send_ends(0, c)

    def first_entry(c):
        if c == 0:
            for copy in rates:
                copy.wait_recv()
        total = entry(0, c)
        enter[cut(c)] = total
        rise[:, cut(c)] = rise[:, cut(c)] + whole[0] * spread(total)
        send_halo(1, c, rise, y_low, y_high)

    def second(c):
        for copy in halos[1, c]:
            copy.wait_recv()
        source = apply_block(coupled(c, y_low, y_high))
        under = jnp.where(
            lane_big == 0, spread(enter[cut(c)]), turn(rise[:, c * wide : (c + 1) * wide], 1)
        )
        value = sweep(source + w_ref[0] * under, 1)
        fall[:, cut(c)] = value
        ends_out[1, cut(c)] = pack(value, 0)
        send_ends(1, c)

    def second_entry(c):
        fall[:, cut(c)] = fall[:, cut(c)] + whole[1] * spread(entry(1, c))

    for work, finish in ((first, first_entry), (second, second_entry)):
        for c in range(n_chunk):
            work(c)
            if c:
                finish(c - 1)
        finish(n_chunk - 1)

    total = jnp.zeros((2 * n_cols, 2 * n_cols), jnp.float32)
    for k in range(n_comp):
        both = jnp.concatenate(split(fall[k]), axis=0)
        total = total + lax.dot_general(
            both, both, (((1,), (1,)), ((), ())), preferred_element_type=jnp.float32
        )
    gram = total[:n_cols] + total[n_cols:]
    gram = gram[:, :n_cols] + gram[:, n_cols:]
    half = n_cols // 2
    packed = jnp.concatenate([gram[:half], gram[half:]], axis=1)
    slot = 0
    for i, peers in enumerate(gram_peers):
        gram_out[i] = packed
        copies = []
        for peer in peers:
            copies.append(
                send(gram_out.at[i], gram_in.at[slot], gram_send.at[slot], gram_recv.at[slot], peer)
            )
            slot += 1
        for j, copy in enumerate(copies):
            copy.wait_recv()
            packed = packed + gram_in[slot - len(copies) + j]
    gram = jnp.concatenate([packed[:, :n_cols], packed[:, n_cols:]], axis=0)

    high, low = split(eliminate(gram) * scale_value)
    left = jnp.concatenate([high, high, low], axis=1)
    for k in range(n_comp):
        top, rest = split(fall[k])
        o_ref[k] = jnp.dot(
            left, jnp.concatenate([top, rest, top], axis=0), preferred_element_type=jnp.float32
        )
    for copy in started:
        copy.wait_send()


def local(n_line, n_tile, forcing, block_inverse, wall_rates, span_couple):
    n_comp, n_cols, n_station, n_point = forcing.shape
    assert n_station == 1
    scale_value = math.sqrt(n_comp * n_station * n_tile * n_point * n_line)
    n_chunk = 4
    phases = reduce_phases(n_line, n_tile)
    n_gram = sum(len(phase_peers(ph, n_line)) for ph in phases)
    n_steps = (n_point - 1).bit_length()
    field = pltpu.VMEM((n_comp, n_cols, n_point), jnp.float32)
    dma = pltpu.SemaphoreType.DMA
    f32 = jnp.float32
    vmem = pl.BlockSpec(memory_space=pltpu.VMEM)
    out = pl.pallas_call(
        functools.partial(kernel, n_line, n_tile, n_chunk, phases, scale_value),
        out_shape=jax.ShapeDtypeStruct((n_comp, n_cols, n_point), f32),
        in_specs=[vmem, vmem, vmem, pl.BlockSpec(memory_space=pltpu.SMEM)],
        out_specs=vmem,
        scratch_shapes=[field] * 7
        + [
            pltpu.VMEM((n_cols, n_point), f32),
            pltpu.VMEM((n_cols, n_point), f32),
            pltpu.VMEM((2, n_cols, n_point), f32),
            pltpu.VMEM((2, n_line - 1, n_cols, n_point), f32),
            pltpu.VMEM((n_cols, n_point), f32),
            pltpu.VMEM((2, ROWS, n_point), f32),
            pltpu.VMEM((n_line - 1, 2, ROWS, n_point), f32),
            pltpu.VMEM((2, n_steps, n_comp, 1, n_point), f32),
            pltpu.VMEM((2, n_comp, 1, n_point), f32),
            pltpu.VMEM((len(phases), n_cols // 2, 2 * n_cols), f32),
            pltpu.VMEM((n_gram, n_cols // 2, 2 * n_cols), f32),
            dma((2, n_chunk, 2)),
            dma((2, n_chunk, 2)),
            dma((n_chunk,)),
            dma((n_chunk,)),
            dma((2, n_chunk, n_line - 1)),
            dma((2, n_chunk, n_line - 1)),
            dma((n_line - 1,)),
            dma((n_line - 1,)),
            dma((n_gram,)),
            dma((n_gram,)),
        ],
        compiler_params=pltpu.CompilerParams(
            collective_id=0, has_side_effects=True, vmem_limit_bytes=32 * 1024 * 1024
        ),
    )(forcing.reshape(n_comp, n_cols, n_point), block_inverse, wall_rates, span_couple)
    return out.reshape(n_comp, n_cols, 1, n_point)


def solution(mesh):
    in_specs = (
        P(None, None, "tile", "line"),
        P(None, None, "tile", "line"),
        P(None, None, "tile", "line"),
        P(),
    )
    out_specs = P(None, None, "tile", "line")
    return jax.shard_map(
        functools.partial(local, mesh.shape["line"], mesh.shape["tile"]),
        mesh=mesh, in_specs=in_specs, out_specs=out_specs, check_vma=False,
    )
```

time: 133 us -> 41.8 us (0.31)
  blocking collectives: 63.6 us -> 0 us
  Pallas kernels: 0 us -> 37.7 us
  other arithmetic: 23.1 us -> 0 us
  local copies, waits for them, and re-layouts: 23.8 us -> 3.86 us
  starting transfers between devices: 14.3 us -> 0 us
  matrix products: 3.47 us -> 0 us
  between operations: 2.5 us -> 0.01 us
    pallas_call x0 -> x1, Pallas kernels: none -> 37.7 us  [local(): pl.pallas_call(functools.partial(kernel, n_line, n_tile, n_chunk, phases,...]
    psum x1 -> x0, blocking collectives: 37 us -> none  [local(): gram = lax.psum(local_gram, ('line', 'tile'))]
    all_gather x2 -> x0, blocking collectives: 15.6 us -> none  [prefix(): everything = jax.tree.map(lambda part: lax.all_gather(part, axis), value)]
    ppermute x9 -> x0, starting transfers between devices: 14.3 us -> none  [the longest x4 12.9 us: with_halo(): lax.ppermute(lax.slice_in_dim(block, 0, width, axis=dim), axis, backward)]
    another operation x5 -> x0, other arithmetic: 12.1 us -> none  [the longest x3 6.52 us: local(): lower_factor = jnp.linalg.cholesky(gram)]
    slice x102 -> x0, local copies, waits for them, and re-layouts: 11.6 us -> none  [the longest x98 10.8 us: local_scan(): lax.associative_scan(compose, (survival_fraction, source), reverse=backwa...]
    unnamed x1 -> x0, blocking collectives: 11.1 us -> none
    add x59 -> x0, other arithmetic: 9.29 us -> none  [the longest x23 2.27 us: compose(): return (earlier[0] * later[0], later[0] * earlier[1] + later[1])]
  transfers between devices with their start and end apart: 9 -> 0, of which waited for: 1 -> 0; matrix products, arithmetic and copies ran while one was open for 7% -> 0% of each run, Pallas kernels for 0% -> 0%
where the time goes in v1:
time: 41.8 us; the launch traced here: 41.5 us
  Pallas kernels  37.7 us (90%)
  local copies, waits for them, and re-layouts  3.86 us (9%)
    pallas_call x1, Pallas kernels, local(): pl.pallas_call(functools.partial(kernel, n_line, n_tile, n_chunk, phases,...  37.7 us
    unnamed x9, local copies, waits for them, and re-layouts  3.86 us

profile of v1, /device:TPU:0, one launch (start us, length us, event | category | flops | bytes accessed | tf_op | source)
XLA Modules:
  0.0 41.5 jit_solution(17373988788807075158)
XLA Ops:
  0.0 0.0 copy-start.3
  0.0 0.7 %copy-done.3 = f32[10]{0:T(128)S(1)} copy-done((f32[10]{0:T(128)S(1)}, f32[10]{0:T(128)}, u32[]{:S(2)}) %copy-start.3) | copy-done | bytes 64
  0.7 0.0 copy-start
  0.7 1.0 %copy-done = f32[10,64,1,128]{3,2,1,0:T(1,128)S(1)} copy-done((f32[10,64,1,128]{3,2,1,0:T(1,128)S(1)}, f32[10,64,1,128]{3,2,1,0:T(1,128)}, u32[]{:S(2)}) %copy-start) | copy-done | bytes 327704
  1.6 0.0 copy-start.1
  1.6 0.8 %copy-done.1 = f32[10,10,1,128]{3,2,1,0:T(1,128)S(1)} copy-done((f32[10,10,1,128]{3,2,1,0:T(1,128)S(1)}, f32[10,10,1,128]{3,2,1,0:T(1,128)}, u32[]{:S(2)}) %copy-start.1) | copy-done | bytes 51224
  2.4 0.0 copy-start.2
  2.4 0.7 %copy-done.2 = f32[2,10,1,128]{3,2,1,0:T(1,128)S(1)} copy-done((f32[2,10,1,128]{3,2,1,0:T(1,128)S(1)}, f32[2,10,1,128]{3,2,1,0:T(1,128)}, u32[]{:S(2)}) %copy-start.2) | copy-done | bytes 10264
  3.1 37.7 %shard_map.46 = f32[10,64,128]{2,1,0:T(8,128)S(1)} custom-call(f32[10,64,128]{2,1,0:T(8,128)S(1)} %bitcast.5, f32[10,10,1,128]{3,2,1,0:T(1,128)S(1)} %copy-done.1, f32[2,10,1,128]{3,2,1,0:T(1,128)S(1)} %copy-done.2, f32[10]{0:T(128)S(1)} %copy-done.3), custom_call_target="tpu_custom_call" | custom-call | tf_op jit(solution)/shard_map/pallas_call | solution.py:303
  40.8 0.7 %copy.7 = f32[10,64,1,128]{3,2,1,0:T(1,128)} copy(f32[10,64,1,128]{3,2,1,0:T(1,128)S(1)} %bitcast.4) | data formatting | bytes 655360
Async XLA Ops:
  0.0 0.7 %copy-start.3 = (f32[10]{0:T(128)S(1)}, f32[10]{0:T(128)}, u32[]{:S(2)}) copy-start(f32[10]{0:T(128)} %s_ref.1) | copy-start | bytes 124
  0.7 1.0 %copy-start = (f32[10,64,1,128]{3,2,1,0:T(1,128)S(1)}, f32[10,64,1,128]{3,2,1,0:T(1,128)}, u32[]{:S(2)}) copy-start(f32[10,64,1,128]{3,2,1,0:T(1,128)} %param.4) | copy-start | bytes 983044
  1.6 0.8 %copy-start.1 = (f32[10,10,1,128]{3,2,1,0:T(1,128)S(1)}, f32[10,10,1,128]{3,2,1,0:T(1,128)}, u32[]{:S(2)}) copy-start(f32[10,10,1,128]{3,2,1,0:T(1,128)} %a_ref.1) | copy-start | bytes 153604
  2.4 0.7 %copy-start.2 = (f32[2,10,1,128]{3,2,1,0:T(1,128)S(1)}, f32[2,10,1,128]{3,2,1,0:T(1,128)}, u32[]{:S(2)}) copy-start(f32[2,10,1,128]{3,2,1,0:T(1,128)} %w_ref.1) | copy-start | bytes 30724

commit v2 on v1

--- a/solution.py
+++ b/solution.py
@@ -35,6 +35,15 @@
     digit = lax.rem(lax.div(tile, stride), factor)
     there = lax.rem(digit + step[1], factor)
     return (lax.rem(line + step[0], n_line), tile + (there - digit) * stride)
+
+
+def scan_strides(n_point):
+    strides, by = [], 1
+    while by < n_point:
+        reach = min(4, -(-n_point // by))
+        strides.append((by, reach))
+        by *= reach
+    return strides
 
 
 def split(value):
@@ -77,12 +86,21 @@
 
 def kernel(
     n_line, n_tile, n_chunk, phases, scale_value,
-    f_ref, a_ref, w_ref, s_ref, o_ref,
+    f_in, a_in, w_in, s_in, o_out,
+    f_ref, a_ref, w_ref, s_ref, o_ref, load_sem, save_sem,
     start, z_low, z_high, rise, y_low, y_high, fall,
     edge_out, edge_in, ends_out, ends_in, enter, rates_out, rates_in, steps, whole,
     gram_out, gram_in, halo_send, halo_recv, edge_send, edge_recv, ends_send, ends_recv,
     rates_send, rates_recv, gram_send, gram_recv,
 ):
+    loads = [
+        pltpu.make_async_copy(src, dst, load_sem.at[i])
+        for i, (src, dst) in enumerate(
+            ((f_in, f_ref), (a_in, a_ref), (w_in, w_ref), (s_in, s_ref))
+        )
+    ]
+    for load in loads:
+        load.start()
     n_comp, n_cols, n_point = f_ref.shape
     wide = n_cols // n_chunk
     line, tile = lax.axis_index("line"), lax.axis_index("tile")
@@ -114,7 +132,7 @@
     lane = lax.broadcasted_iota(jnp.int32, (wide, n_point), 1)
     lane8 = lax.broadcasted_iota(jnp.int32, (ROWS, n_point), 1)
     lane_big = lax.broadcasted_iota(jnp.int32, (n_comp, wide, n_point), 2)
-    n_steps = (n_point - 1).bit_length()
+    strides = scan_strides(n_point)
 
     def turn(value, by):
         flat = value.reshape(-1, n_point)
@@ -139,9 +157,12 @@
         )
 
     def sweep(value, side):
-        for i in range(n_steps):
-            by = 1 << i
-            value = value + steps[side, i] * turn(value, -by if side else by)
+        slot = 0
+        for by, reach in strides:
+            parts = [turn(value, -by * m if side else by * m) for m in range(1, reach)]
+            for part in parts:
+                value = value + steps[side, slot] * part
+                slot += 1
         return value
 
     halos = {}
@@ -162,6 +183,8 @@
             for d, peer in enumerate(line_peers)
         ]
 
+    for load in loads:
+        load.wait()
     for c in range(n_chunk):
         field = apply_block(f_ref[:, c * wide : (c + 1) * wide])
         start[:, cut(c)] = field
@@ -175,11 +198,14 @@
 
     for side in range(2):
         rate = w_ref[side]
-        for i in range(n_steps):
-            by = 1 << i
-            inside = lane3 < n_point - by if side else lane3 >= by
-            steps[side, i] = jnp.where(inside, rate, 0.0)
-            rate = rate * jnp.where(inside, turn(rate, -by if side else by), 1.0)
+        slot = 0
+        for by, reach in strides:
+            parts = [rate]
+            for m in range(1, reach):
+                inside = lane3 < n_point - by * m if side else lane3 >= by * m
+                steps[side, slot] = jnp.where(inside, rate, 0.0)
+                slot += 1
+                rate = rate * jnp.where(inside, turn(parts[0], -by * m if side else by * m), 1.0)
         whole[side] = rate
         at = 0 if side else n_point - 1
         total = jnp.zeros((ROWS, n_point), jnp.float32)
@@ -279,11 +305,16 @@
 
     high, low = split(eliminate(gram) * scale_value)
     left = jnp.concatenate([high, high, low], axis=1)
+    saves = []
     for k in range(n_comp):
         top, rest = split(fall[k])
         o_ref[k] = jnp.dot(
             left, jnp.concatenate([top, rest, top], axis=0), preferred_element_type=jnp.float32
         )
+        saves.append(pltpu.make_async_copy(o_ref.at[k], o_out.at[k], save_sem.at[k]))
+        saves[k].start()
+    for save in saves:
+        save.wait()
     for copy in started:
         copy.wait_send()
 
@@ -295,17 +326,25 @@
     n_chunk = 4
     phases = reduce_phases(n_line, n_tile)
     n_gram = sum(len(phase_peers(ph, n_line)) for ph in phases)
-    n_steps = (n_point - 1).bit_length()
+    n_steps = sum(reach - 1 for _, reach in scan_strides(n_point))
     field = pltpu.VMEM((n_comp, n_cols, n_point), jnp.float32)
     dma = pltpu.SemaphoreType.DMA
     f32 = jnp.float32
-    vmem = pl.BlockSpec(memory_space=pltpu.VMEM)
     out = pl.pallas_call(
         functools.partial(kernel, n_line, n_tile, n_chunk, phases, scale_value),
         out_shape=jax.ShapeDtypeStruct((n_comp, n_cols, n_point), f32),
-        in_specs=[vmem, vmem, vmem, pl.BlockSpec(memory_space=pltpu.SMEM)],
-        out_specs=vmem,
-        scratch_shapes=[field] * 7
+        in_specs=[pl.BlockSpec(memory_space=pltpu.HBM)] * 4,
+        out_specs=pl.BlockSpec(memory_space=pltpu.HBM),
+        scratch_shapes=[
+            field,
+            pltpu.VMEM(block_inverse.shape, f32),
+            pltpu.VMEM(wall_rates.shape, f32),
+            pltpu.SMEM(span_couple.shape, f32),
+            field,
+            dma((4,)),
+            dma((n_comp,)),
+        ]
+        + [field] * 7
         + [
             pltpu.VMEM((n_cols, n_point), f32),
             pltpu.VMEM((n_cols, n_point), f32),
@@ -330,7 +369,7 @@
             dma((n_gram,)),
         ],
         compiler_params=pltpu.CompilerParams(
-            collective_id=0, has_side_effects=True, vmem_limit_bytes=32 * 1024 * 1024
+            collective_id=0, has_side_effects=True, vmem_limit_bytes=64 * 1024 * 1024
         ),
     )(forcing.reshape(n_comp, n_cols, n_point), block_inverse, wall_rates, span_couple)
     return out.reshape(n_comp, n_cols, 1, n_point)

time: 41.8 us -> 39.4 us (0.943)
  local copies, waits for them, and re-layouts: 3.86 us -> 1.72 us
    unnamed x9 -> x1, local copies, waits for them, and re-layouts: 3.86 us -> 1.72 us
where the time goes in v2:
time: 39.4 us; the launch traced here: 39.2 us
  Pallas kernels  37.5 us (95%)
  local copies, waits for them, and re-layouts  1.72 us (4%)
    pallas_call x1, Pallas kernels, local(): pl.pallas_call(functools.partial(kernel, n_line, n_tile, n_chunk, phases,...  37.5 us
    unnamed x1, local copies, waits for them, and re-layouts  1.72 us

profile of v2, /device:TPU:0, one launch (start us, length us, event | category | flops | bytes accessed | tf_op | source)
XLA Modules:
  0.0 39.2 jit_solution(3938139742866265352)
XLA Ops:
  0.0 37.5 %shard_map.46 = f32[10,64,128]{2,1,0:T(8,128)} custom-call(f32[10,64,128]{2,1,0:T(8,128)} %bitcast.5, f32[10,10,1,128]{3,2,1,0:T(1,128)} %a_in.1, f32[2,10,1,128]{3,2,1,0:T(1,128)} %w_in.1, f32[10]{0:T(128)} %s_in.1), custom_call_target="tpu_custom_call" | custom-call | tf_op jit(solution)/shard_map/pallas_call | solution.py:333
  37.5 1.7 %copy.7 = f32[10,64,1,128]{3,2,1,0:T(1,128)} copy(f32[10,64,1,128]{3,2,1,0:T(1,128)} %bitcast.4) | data formatting | bytes 655360

commit v3 on v2

--- a/solution.py
+++ b/solution.py
@@ -52,45 +52,40 @@
     return high, low
 
 
-def eliminate(gram):
-    n = gram.shape[0]
-    row = lax.broadcasted_iota(jnp.int32, (n, n), 0)
-    col = lax.broadcasted_iota(jnp.int32, (n, n), 1)
-    both = jnp.concatenate([gram, (row == col).astype(jnp.float32)], axis=1)
-    blocks = [both[v * ROWS : (v + 1) * ROWS] for v in range(n // ROWS)]
-    shape = (ROWS, 2 * n)
+def eliminate(square, right):
+    n, shape = square.shape[0], (ROWS, right.shape[1])
+    groups = n // ROWS
     sub = lax.broadcasted_iota(jnp.int32, shape, 0)
-    scales = []
-    for q in range(n // ROWS):
-        live = range(q, n // ROWS)
-        cols = [
-            {v: jnp.broadcast_to(blocks[v][:, ROWS * q + c : ROWS * q + c + 1], shape) for v in live}
-            for c in range(ROWS)
-        ]
-        scale = jnp.zeros(shape, jnp.float32)
-        for c in range(ROWS):
-            pivot = jnp.broadcast_to(cols[c][q][c : c + 1], shape)
-            inv = 1.0 / pivot
-            scale = jnp.where(sub == c, lax.rsqrt(pivot), scale)
-            factor = {v: cols[c][v] * inv for v in live}
-            factor[q] = jnp.where(sub > c, factor[q], 0.0)
-            top = jnp.broadcast_to(blocks[q][c : c + 1], shape)
-            tops = [jnp.broadcast_to(cols[e][q][c : c + 1], shape) for e in range(c + 1, ROWS)]
-            for v in live:
-                blocks[v] = blocks[v] - factor[v] * top
-                for e in range(c + 1, ROWS):
-                    cols[e][v] = cols[e][v] - factor[v] * tops[e - c - 1]
-        scales.append(scale)
-    return jnp.concatenate([b * s for b, s in zip(blocks, scales)], axis=0)[:, n:]
+    blocks = [right[v * ROWS : (v + 1) * ROWS] for v in range(groups)]
+    cols = [
+        [jnp.broadcast_to(square[v * ROWS : (v + 1) * ROWS, e : e + 1], shape) for v in range(groups)]
+        for e in range(n)
+    ]
+    scales = [jnp.zeros(shape, jnp.float32)] * groups
+    for p in range(n):
+        q, c = divmod(p, ROWS)
+        pivot = jnp.broadcast_to(cols[p][q][c : c + 1], shape)
+        inv = 1.0 / pivot
+        scales[q] = jnp.where(sub == c, lax.rsqrt(pivot), scales[q])
+        top = jnp.broadcast_to(blocks[q][c : c + 1], shape)
+        tops = {e: jnp.broadcast_to(cols[e][q][c : c + 1], shape) for e in range(p + 1, n)}
+        for v in range(q, groups):
+            factor = cols[p][v] * inv
+            if v == q:
+                factor = jnp.where(sub > c, factor, 0.0)
+            blocks[v] = blocks[v] - factor * top
+            for e in range(p + 1, n):
+                cols[e][v] = cols[e][v] - factor * tops[e]
+    return jnp.concatenate([b * t for b, t in zip(blocks, scales)], axis=0)
 
 
 def kernel(
     n_line, n_tile, n_chunk, phases, scale_value,
-    f_in, a_in, w_in, s_in, o_out,
-    f_ref, a_ref, w_ref, s_ref, o_ref, load_sem, save_sem,
+    f_in, a_in, w_in, s_in, o_ref,
+    f_ref, a_ref, w_ref, s_ref, load_sem,
     start, z_low, z_high, rise, y_low, y_high, fall,
     edge_out, edge_in, ends_out, ends_in, enter, rates_out, rates_in, steps, whole,
-    gram_out, gram_in, halo_send, halo_recv, edge_send, edge_recv, ends_send, ends_recv,
+    high, low, gram_out, gram_in, halo_send, halo_recv, edge_send, edge_recv, ends_send, ends_recv,
     rates_send, rates_recv, gram_send, gram_recv,
 ):
     loads = [
@@ -272,49 +267,94 @@
     def second_entry(c):
         fall[:, cut(c)] = fall[:, cut(c)] + whole[1] * spread(entry(1, c))
 
-    for work, finish in ((first, first_entry), (second, second_entry)):
-        for c in range(n_chunk):
-            work(c)
-            if c:
-                finish(c - 1)
-        finish(n_chunk - 1)
-
-    total = jnp.zeros((2 * n_cols, 2 * n_cols), jnp.float32)
-    for k in range(n_comp):
-        both = jnp.concatenate(split(fall[k]), axis=0)
-        total = total + lax.dot_general(
-            both, both, (((1,), (1,)), ((), ())), preferred_element_type=jnp.float32
-        )
-    gram = total[:n_cols] + total[n_cols:]
-    gram = gram[:, :n_cols] + gram[:, n_cols:]
-    half = n_cols // 2
-    packed = jnp.concatenate([gram[:half], gram[half:]], axis=1)
-    slot = 0
-    for i, peers in enumerate(gram_peers):
-        gram_out[i] = packed
-        copies = []
-        for peer in peers:
-            copies.append(
-                send(gram_out.at[i], gram_in.at[slot], gram_send.at[slot], gram_recv.at[slot], peer)
-            )
-            slot += 1
-        for j, copy in enumerate(copies):
+    def panel(c):
+        till = (c + 1) * wide
+        parts = [split(fall[k, cut(c)]) for k in range(n_comp)]
+        for k, (top, rest) in enumerate(parts):
+            high[k, cut(c)], low[k, cut(c)] = top, rest
+        tops = jnp.concatenate([top for top, _ in parts], axis=1)
+        left = jnp.concatenate([tops, jnp.concatenate([rest for _, rest in parts], axis=1)], axis=0)
+        both = lax.dot_general(
+            left, jnp.concatenate([high[k, :till] for k in range(n_comp)], axis=1),
+            (((1,), (1,)), ((), ())), preferred_element_type=jnp.float32,
+        )
+        cross = lax.dot_general(
+            tops, jnp.concatenate([low[k, :till] for k in range(n_comp)], axis=1),
+            (((1,), (1,)), ((), ())), preferred_element_type=jnp.float32,
+        )
+        rows = both[:wide] + both[wide:] + cross
+        if till < n_cols:
+            rows = jnp.concatenate([rows, jnp.zeros((wide, n_cols - till), jnp.float32)], axis=1)
+        return jnp.concatenate([rows[: wide // 2], rows[wide // 2 :]], axis=1)
+
+    sums, flights, factor_rows = {}, {}, []
+
+    def gram_send_phase(c, i):
+        gram_out[c, i] = sums[c]
+        slot = sum(len(peers) for peers in gram_peers[:i])
+        flights[c] = []
+        for j, peer in enumerate(gram_peers[i]):
+            at = slot + j
+            copy = send(gram_out.at[c, i], gram_in.at[c, at], gram_send.at[c, at],
+                        gram_recv.at[c, at], peer)
+            flights[c].append((copy, at))
+
+    def gram_collect(c):
+        for copy, at in flights[c]:
             copy.wait_recv()
-            packed = packed + gram_in[slot - len(copies) + j]
-    gram = jnp.concatenate([packed[:, :n_cols], packed[:, n_cols:]], axis=0)
-
-    high, low = split(eliminate(gram) * scale_value)
-    left = jnp.concatenate([high, high, low], axis=1)
-    saves = []
-    for k in range(n_comp):
-        top, rest = split(fall[k])
-        o_ref[k] = jnp.dot(
-            left, jnp.concatenate([top, rest, top], axis=0), preferred_element_type=jnp.float32
-        )
-        saves.append(pltpu.make_async_copy(o_ref.at[k], o_out.at[k], save_sem.at[k]))
-        saves[k].start()
-    for save in saves:
-        save.wait()
+            sums[c] = sums[c] + gram_in[c, at]
+
+    def dot(left, right, transposed):
+        return lax.dot_general(
+            left, right, (((1,), (1 if transposed else 0,)), ((), ())),
+            precision=lax.Precision.HIGHEST, preferred_element_type=jnp.float32,
+        )
+
+    def factor(c):
+        from_col, till = c * wide, (c + 1) * wide
+        rows = jnp.concatenate([sums[c][:, :n_cols], sums[c][:, n_cols:]], axis=0)
+        square = rows[:, from_col:till]
+        row = lax.broadcasted_iota(jnp.int32, (wide, n_cols), 0)
+        col = lax.broadcasted_iota(jnp.int32, (wide, n_cols), 1)
+        right = (col == row + from_col).astype(jnp.float32)
+        if c:
+            known = jnp.concatenate(factor_rows, axis=0)
+            lower = dot(rows, known, True)
+            square = square - dot(lower, lower, True)
+            right = right - dot(lower, known, False)
+        factor_rows.append(eliminate(square, right))
+        top, rest = split(factor_rows[c][:, :till] * scale_value)
+        left = jnp.concatenate([top, rest], axis=0)
+        for k in range(n_comp):
+            both = jnp.dot(left, high[k, :till], preferred_element_type=jnp.float32)
+            cross = jnp.dot(top, low[k, :till], preferred_element_type=jnp.float32)
+            o_ref[k, cut(c)] = both[:wide] + both[wide:] + cross
+
+    for c in range(n_chunk):
+        first(c)
+        if c:
+            first_entry(c - 1)
+    first_entry(n_chunk - 1)
+
+    def stage(c, which):
+        if which == 0:
+            second(c)
+            return
+        if which == 1:
+            second_entry(c)
+            sums[c] = panel(c)
+        else:
+            gram_collect(c)
+        if which <= len(phases):
+            gram_send_phase(c, which - 1)
+        else:
+            factor(c)
+
+    n_stages = len(phases) + 2
+    for now in range(n_chunk + n_stages - 1):
+        for c in range(min(now, n_chunk - 1), -1, -1):
+            if now - c < n_stages:
+                stage(c, now - c)
     for copy in started:
         copy.wait_send()
 
@@ -324,25 +364,25 @@
     assert n_station == 1
     scale_value = math.sqrt(n_comp * n_station * n_tile * n_point * n_line)
     n_chunk = 4
+    half = n_cols // n_chunk // 2
     phases = reduce_phases(n_line, n_tile)
     n_gram = sum(len(phase_peers(ph, n_line)) for ph in phases)
     n_steps = sum(reach - 1 for _, reach in scan_strides(n_point))
     field = pltpu.VMEM((n_comp, n_cols, n_point), jnp.float32)
     dma = pltpu.SemaphoreType.DMA
     f32 = jnp.float32
+    inputs = (forcing.reshape(n_comp, n_cols, n_point), block_inverse, wall_rates, span_couple)
     out = pl.pallas_call(
         functools.partial(kernel, n_line, n_tile, n_chunk, phases, scale_value),
-        out_shape=jax.ShapeDtypeStruct((n_comp, n_cols, n_point), f32),
+        out_shape=pltpu.VMEM((n_comp, n_cols, n_point), f32),
         in_specs=[pl.BlockSpec(memory_space=pltpu.HBM)] * 4,
-        out_specs=pl.BlockSpec(memory_space=pltpu.HBM),
+        out_specs=pl.BlockSpec(memory_space=pltpu.VMEM),
         scratch_shapes=[
             field,
             pltpu.VMEM(block_inverse.shape, f32),
             pltpu.VMEM(wall_rates.shape, f32),
             pltpu.SMEM(span_couple.shape, f32),
-            field,
             dma((4,)),
-            dma((n_comp,)),
         ]
         + [field] * 7
         + [
@@ -355,8 +395,10 @@
             pltpu.VMEM((n_line - 1, 2, ROWS, n_point), f32),
             pltpu.VMEM((2, n_steps, n_comp, 1, n_point), f32),
             pltpu.VMEM((2, n_comp, 1, n_point), f32),
-            pltpu.VMEM((len(phases), n_cols // 2, 2 * n_cols), f32),
-            pltpu.VMEM((n_gram, n_cols // 2, 2 * n_cols), f32),
+            pltpu.VMEM((n_comp, n_cols, n_point), jnp.bfloat16),
+            pltpu.VMEM((n_comp, n_cols, n_point), jnp.bfloat16),
+            pltpu.VMEM((n_chunk, len(phases), half, 2 * n_cols), f32),
+            pltpu.VMEM((n_chunk, n_gram, half, 2 * n_cols), f32),
             dma((2, n_chunk, 2)),
             dma((2, n_chunk, 2)),
             dma((n_chunk,)),
@@ -365,13 +407,13 @@
             dma((2, n_chunk, n_line - 1)),
             dma((n_line - 1,)),
             dma((n_line - 1,)),
-            dma((n_gram,)),
-            dma((n_gram,)),
+            dma((n_chunk, n_gram)),
+            dma((n_chunk, n_gram)),
         ],
         compiler_params=pltpu.CompilerParams(
-            collective_id=0, has_side_effects=True, vmem_limit_bytes=64 * 1024 * 1024
+            collective_id=0, has_side_effects=True, vmem_limit_bytes=32 * 1024 * 1024
         ),
-    )(forcing.reshape(n_comp, n_cols, n_point), block_inverse, wall_rates, span_couple)
+    )(*[pltpu.with_memory_space_constraint(value, pltpu.HBM) for value in inputs])
     return out.reshape(n_comp, n_cols, 1, n_point)
 
 

time: 39.4 us -> 40.7 us (1.033)
  Pallas kernels: 37.5 us -> 39.8 us
  local copies, waits for them, and re-layouts: 1.72 us -> 0.73 us
    pallas_call x1, Pallas kernels: 37.5 us -> 39.8 us  [local(): pl.pallas_call(functools.partial(kernel, n_line, n_tile, n_chunk, phases,...]
    unnamed x1, local copies, waits for them, and re-layouts: 1.72 us -> 0.73 us
where the time goes in v3:
time: 40.7 us; the launch traced here: 40.6 us
  Pallas kernels  39.8 us (98%)
  local copies, waits for them, and re-layouts  0.73 us (2%)
    pallas_call x1, Pallas kernels, local(): pl.pallas_call(functools.partial(kernel, n_line, n_tile, n_chunk, phases,...  39.8 us

profile of v3, /device:TPU:0, one launch (start us, length us, event | category | flops | bytes accessed | tf_op | source)
XLA Modules:
  0.0 40.6 jit_solution(3691244982316488769)
XLA Ops:
  0.0 39.8 %shard_map.46 = f32[10,64,128]{2,1,0:T(8,128)S(1)} custom-call(f32[10,64,128]{2,1,0:T(8,128)} %bitcast.5, f32[10,10,1,128]{3,2,1,0:T(1,128)} %a_in.1, f32[2,10,1,128]{3,2,1,0:T(1,128)} %w_in.1, f32[10]{0:T(128)} %s_in.1), custom_call_target="tpu_custom_call" | custom-call | tf_op jit(solution)/shard_map/pallas_call | solution.py:375
  39.8 0.7 %copy.7 = f32[10,64,1,128]{3,2,1,0:T(1,128)} copy(f32[10,64,1,128]{3,2,1,0:T(1,128)S(1)} %bitcast.4) | data formatting | bytes 655360

commit v4 on v3

--- a/solution.py
+++ b/solution.py
@@ -363,7 +363,7 @@
     n_comp, n_cols, n_station, n_point = forcing.shape
     assert n_station == 1
     scale_value = math.sqrt(n_comp * n_station * n_tile * n_point * n_line)
-    n_chunk = 4
+    n_chunk = 2
     half = n_cols // n_chunk // 2
     phases = reduce_phases(n_line, n_tile)
     n_gram = sum(len(phase_peers(ph, n_line)) for ph in phases)

time: 40.7 us -> 38.3 us (0.941)
  Pallas kernels: 39.8 us -> 37.4 us
    pallas_call x1, Pallas kernels: 39.8 us -> 37.4 us  [local(): pl.pallas_call(functools.partial(kernel, n_line, n_tile, n_chunk, phases,...]
where the time goes in v4:
time: 38.3 us; the launch traced here: 38.2 us
  Pallas kernels  37.4 us (98%)
  local copies, waits for them, and re-layouts  0.73 us (2%)
    pallas_call x1, Pallas kernels, local(): pl.pallas_call(functools.partial(kernel, n_line, n_tile, n_chunk, phases,...  37.4 us

profile of v4, /device:TPU:0, one launch (start us, length us, event | category | flops | bytes accessed | tf_op | source)
XLA Modules:
  0.0 38.2 jit_solution(11889398889192025775)
XLA Ops:
  0.0 37.4 %shard_map.46 = f32[10,64,128]{2,1,0:T(8,128)S(1)} custom-call(f32[10,64,128]{2,1,0:T(8,128)} %bitcast.5, f32[10,10,1,128]{3,2,1,0:T(1,128)} %a_in.1, f32[2,10,1,128]{3,2,1,0:T(1,128)} %w_in.1, f32[10]{0:T(128)} %s_in.1), custom_call_target="tpu_custom_call" | custom-call | tf_op jit(solution)/shard_map/pallas_call | solution.py:375
  37.4 0.7 %copy.7 = f32[10,64,1,128]{3,2,1,0:T(1,128)} copy(f32[10,64,1,128]{3,2,1,0:T(1,128)S(1)} %bitcast.4) | data formatting | bytes 655360

commit v5 on v4

--- a/solution.py
+++ b/solution.py
@@ -46,41 +46,73 @@
     return strides
 
 
+def chunk_widths(n_cols):
+    return [n_cols // 2, n_cols // 4, n_cols // 4]
+
+
 def split(value):
     high = value.astype(jnp.bfloat16)
     low = (value - high.astype(jnp.float32)).astype(jnp.bfloat16)
     return high, low
 
 
+def inverse_of(value):
+    guess = pl.reciprocal(value, approx=True)
+    guess = guess * (2.0 - value * guess)
+    return guess * (2.0 - value * guess)
+
+
 def eliminate(square, right):
     n, shape = square.shape[0], (ROWS, right.shape[1])
     groups = n // ROWS
     sub = lax.broadcasted_iota(jnp.int32, shape, 0)
+
+    def every(block, at):
+        return jnp.broadcast_to(block[at : at + 1], shape)
+
     blocks = [right[v * ROWS : (v + 1) * ROWS] for v in range(groups)]
     cols = [
-        [jnp.broadcast_to(square[v * ROWS : (v + 1) * ROWS, e : e + 1], shape) for v in range(groups)]
-        for e in range(n)
+        [
+            jnp.broadcast_to(square[v * ROWS : (v + 1) * ROWS, e : e + 1], shape)
+            for e in range((v + 1) * ROWS)
+        ]
+        for v in range(groups)
     ]
-    scales = [jnp.zeros(shape, jnp.float32)] * groups
-    for p in range(n):
-        q, c = divmod(p, ROWS)
-        pivot = jnp.broadcast_to(cols[p][q][c : c + 1], shape)
-        inv = 1.0 / pivot
-        scales[q] = jnp.where(sub == c, lax.rsqrt(pivot), scales[q])
-        top = jnp.broadcast_to(blocks[q][c : c + 1], shape)
-        tops = {e: jnp.broadcast_to(cols[e][q][c : c + 1], shape) for e in range(p + 1, n)}
-        for v in range(q, groups):
-            factor = cols[p][v] * inv
-            if v == q:
-                factor = jnp.where(sub > c, factor, 0.0)
-            blocks[v] = blocks[v] - factor * top
-            for e in range(p + 1, n):
-                cols[e][v] = cols[e][v] - factor * tops[e]
-    return jnp.concatenate([b * t for b, t in zip(blocks, scales)], axis=0)
+    for q in range(groups):
+        base = q * ROWS
+        cell = {(i, j): every(cols[q][base + j], i) for i in range(ROWS) for j in range(i + 1)}
+        lines = [every(blocks[q], i) for i in range(ROWS)]
+        later = range(q + 1, groups)
+        shares = {}
+        for c in range(ROWS):
+            inv = inverse_of(cell[c, c])
+            for i in range(c + 1, ROWS):
+                share = cell[i, c] * inv
+                for j in range(c + 1, i + 1):
+                    cell[i, j] = cell[i, j] - share * cell[j, c]
+                lines[i] = lines[i] - share * lines[c]
+            for v in later:
+                share = cols[v][base + c] * inv
+                shares[v, c] = share
+                for j in range(c + 1, ROWS):
+                    cols[v][base + j] = cols[v][base + j] - share * cell[j, c]
+                blocks[v] = blocks[v] - share * lines[c]
+        done = lines[0] * lax.rsqrt(cell[0, 0])
+        for i in range(1, ROWS):
+            done = jnp.where(sub == i, lines[i] * lax.rsqrt(cell[i, i]), done)
+        blocks[q] = done
+        for w in later:
+            for c in range(ROWS):
+                for e in range(ROWS):
+                    top = every(cols[w][base + c], e)
+                    for v in range(w, groups):
+                        at = w * ROWS + e
+                        cols[v][at] = cols[v][at] - shares[v, c] * top
+    return jnp.concatenate(blocks, axis=0)
 
 
 def kernel(
-    n_line, n_tile, n_chunk, phases, scale_value,
+    n_line, n_tile, widths, phases, scale_value,
     f_in, a_in, w_in, s_in, o_ref,
     f_ref, a_ref, w_ref, s_ref, load_sem,
     start, z_low, z_high, rise, y_low, y_high, fall,
@@ -97,7 +129,9 @@
     for load in loads:
         load.start()
     n_comp, n_cols, n_point = f_ref.shape
-    wide = n_cols // n_chunk
+    n_chunk = len(widths)
+    begins = [sum(widths[:c]) for c in range(n_chunk)]
+    ends_at = [sum(widths[: c + 1]) for c in range(n_chunk)]
     line, tile = lax.axis_index("line"), lax.axis_index("tile")
     above, below = lax.rem(tile + 1, n_tile), lax.rem(tile + n_tile - 1, n_tile)
     line_peers = [(lax.rem(line + d, n_line), tile) for d in range(1, n_line)]
@@ -121,12 +155,10 @@
         return copy
 
     def cut(c):
-        return pl.ds(c * wide, wide)
+        return pl.ds(begins[c], widths[c])
 
     lane3 = lax.broadcasted_iota(jnp.int32, (n_comp, 1, n_point), 2)
-    lane = lax.broadcasted_iota(jnp.int32, (wide, n_point), 1)
     lane8 = lax.broadcasted_iota(jnp.int32, (ROWS, n_point), 1)
-    lane_big = lax.broadcasted_iota(jnp.int32, (n_comp, wide, n_point), 2)
     strides = scan_strides(n_point)
 
     def turn(value, by):
@@ -148,7 +180,7 @@
 
     def spread(packed):
         return jnp.stack(
-            [jnp.broadcast_to(packed[:, k : k + 1], (wide, n_point)) for k in range(n_comp)], axis=0
+            [jnp.broadcast_to(packed[:, k : k + 1], packed.shape) for k in range(n_comp)], axis=0
         )
 
     def sweep(value, side):
@@ -181,7 +213,7 @@
     for load in loads:
         load.wait()
     for c in range(n_chunk):
-        field = apply_block(f_ref[:, c * wide : (c + 1) * wide])
+        field = apply_block(f_ref[:, begins[c] : ends_at[c]])
         start[:, cut(c)] = field
         edge_out[cut(c)] = pack(field, 0)
         if c == 0:
@@ -211,15 +243,15 @@
         rates.append(send(rates_out, rates_in.at[d], rates_send.at[d], rates_recv.at[d], peer))
 
     def coupled(c, low, high):
-        beside = low[:, c * wide : (c + 1) * wide] + high[:, c * wide : (c + 1) * wide]
+        beside = low[:, begins[c] : ends_at[c]] + high[:, begins[c] : ends_at[c]]
         return jnp.stack(
-            [f_ref[k, c * wide : (c + 1) * wide] + s_ref[k] * beside[k] for k in range(n_comp)], axis=0
+            [f_ref[k, begins[c] : ends_at[c]] + s_ref[k] * beside[k] for k in range(n_comp)], axis=0
         )
 
     def entry(which, c):
         for copy in ends[which, c]:
             copy.wait_recv()
-        total = jnp.zeros((wide, n_point), jnp.float32)
+        total = jnp.zeros((widths[c], n_point), jnp.float32)
         carried = jnp.ones((1, n_point), jnp.float32)
         for d in range(1, n_line):
             slot = n_line - d - 1 if which else d - 1
@@ -235,8 +267,8 @@
         source = apply_block(coupled(c, z_low, z_high))
         last = (line < n_line - 1).astype(jnp.float32)
         over = jnp.where(
-            lane_big == n_point - 1, spread(edge_in[cut(c)] * last),
-            turn(start[:, c * wide : (c + 1) * wide], -1),
+            lane3 == n_point - 1, spread(edge_in[cut(c)] * last),
+            turn(start[:, begins[c] : ends_at[c]], -1),
         )
         value = sweep(source + w_ref[1] * over, 0)
         rise[:, cut(c)] = value
@@ -257,7 +289,7 @@
             copy.wait_recv()
         source = apply_block(coupled(c, y_low, y_high))
         under = jnp.where(
-            lane_big == 0, spread(enter[cut(c)]), turn(rise[:, c * wide : (c + 1) * wide], 1)
+            lane3 == 0, spread(enter[cut(c)]), turn(rise[:, begins[c] : ends_at[c]], 1)
         )
         value = sweep(source + w_ref[0] * under, 1)
         fall[:, cut(c)] = value
@@ -268,7 +300,7 @@
         fall[:, cut(c)] = fall[:, cut(c)] + whole[1] * spread(entry(1, c))
 
     def panel(c):
-        till = (c + 1) * wide
+        wide, till = widths[c], ends_at[c]
         parts = [split(fall[k, cut(c)]) for k in range(n_comp)]
         for k, (top, rest) in enumerate(parts):
             high[k, cut(c)], low[k, cut(c)] = top, rest
@@ -290,19 +322,20 @@
     sums, flights, factor_rows = {}, {}, []
 
     def gram_send_phase(c, i):
-        gram_out[c, i] = sums[c]
+        rows = pl.ds(0, widths[c] // 2)
+        gram_out[c, i, rows] = sums[c]
         slot = sum(len(peers) for peers in gram_peers[:i])
         flights[c] = []
         for j, peer in enumerate(gram_peers[i]):
             at = slot + j
-            copy = send(gram_out.at[c, i], gram_in.at[c, at], gram_send.at[c, at],
+            copy = send(gram_out.at[c, i, rows], gram_in.at[c, at, rows], gram_send.at[c, at],
                         gram_recv.at[c, at], peer)
             flights[c].append((copy, at))
 
     def gram_collect(c):
         for copy, at in flights[c]:
             copy.wait_recv()
-            sums[c] = sums[c] + gram_in[c, at]
+            sums[c] = sums[c] + gram_in[c, at, : widths[c] // 2]
 
     def dot(left, right, transposed):
         return lax.dot_general(
@@ -311,7 +344,7 @@
         )
 
     def factor(c):
-        from_col, till = c * wide, (c + 1) * wide
+        wide, from_col, till = widths[c], begins[c], ends_at[c]
         rows = jnp.concatenate([sums[c][:, :n_cols], sums[c][:, n_cols:]], axis=0)
         square = rows[:, from_col:till]
         row = lax.broadcasted_iota(jnp.int32, (wide, n_cols), 0)
@@ -363,8 +396,8 @@
     n_comp, n_cols, n_station, n_point = forcing.shape
     assert n_station == 1
     scale_value = math.sqrt(n_comp * n_station * n_tile * n_point * n_line)
-    n_chunk = 2
-    half = n_cols // n_chunk // 2
+    widths = chunk_widths(n_cols)
+    n_chunk, half = len(widths), max(widths) // 2
     phases = reduce_phases(n_line, n_tile)
     n_gram = sum(len(phase_peers(ph, n_line)) for ph in phases)
     n_steps = sum(reach - 1 for _, reach in scan_strides(n_point))
@@ -373,7 +406,7 @@
     f32 = jnp.float32
     inputs = (forcing.reshape(n_comp, n_cols, n_point), block_inverse, wall_rates, span_couple)
     out = pl.pallas_call(
-        functools.partial(kernel, n_line, n_tile, n_chunk, phases, scale_value),
+        functools.partial(kernel, n_line, n_tile, widths, phases, scale_value),
         out_shape=pltpu.VMEM((n_comp, n_cols, n_point), f32),
         in_specs=[pl.BlockSpec(memory_space=pltpu.HBM)] * 4,
         out_specs=pl.BlockSpec(memory_space=pltpu.VMEM),

time: 38.3 us -> 40.4 us (1.055)
  Pallas kernels: 37.4 us -> 39.5 us
    pallas_call x1, Pallas kernels: 37.4 us -> 39.5 us  [local(): pl.pallas_call(functools.partial(kernel, n_line, n_tile, widths, phases,...]
where the time goes in v5:
time: 40.4 us; the launch traced here: 40.3 us
  Pallas kernels  39.5 us (98%)
  local copies, waits for them, and re-layouts  0.73 us (2%)
    pallas_call x1, Pallas kernels, local(): pl.pallas_call(functools.partial(kernel, n_line, n_tile, widths, phases,...  39.5 us

profile of v5, /device:TPU:0, one launch (start us, length us, event | category | flops | bytes accessed | tf_op | source)
XLA Modules:
  0.0 40.3 jit_solution(9638100628205262094)
XLA Ops:
  0.0 39.5 %shard_map.46 = f32[10,64,128]{2,1,0:T(8,128)S(1)} custom-call(f32[10,64,128]{2,1,0:T(8,128)} %bitcast.5, f32[10,10,1,128]{3,2,1,0:T(1,128)} %a_in.1, f32[2,10,1,128]{3,2,1,0:T(1,128)} %w_in.1, f32[10]{0:T(128)} %s_in.1), custom_call_target="tpu_custom_call" | custom-call | tf_op jit(solution)/shard_map/pallas_call | solution.py:408
  39.5 0.7 %copy.7 = f32[10,64,1,128]{3,2,1,0:T(1,128)} copy(f32[10,64,1,128]{3,2,1,0:T(1,128)S(1)} %bitcast.4) | data formatting | bytes 655360

commit v6 on v5

--- a/solution.py
+++ b/solution.py
@@ -47,7 +47,7 @@
 
 
 def chunk_widths(n_cols):
-    return [n_cols // 2, n_cols // 4, n_cols // 4]
+    return [n_cols // 2, n_cols // 2]
 
 
 def split(value):
@@ -138,6 +138,7 @@
     lower_line = (lax.rem(line + n_line - 1, n_line), tile)
     gram_peers = [[peer_id(ph, step, n_line) for step in phase_peers(ph, n_line)] for ph in phases]
 
+    ends_in[...] = jnp.zeros(ends_in.shape, jnp.float32)
     greet = [(line, above), (line, below)] + [p for peers in gram_peers for p in peers]
     barrier = pltpu.get_barrier_semaphore()
     for peer in greet:
@@ -193,7 +194,7 @@
         return value
 
     halos = {}
-    edges, ends, rates = [], {}, []
+    edges, rates = [], []
 
     def send_halo(which, c, field, low, high):
         halos[which, c] = [
@@ -203,12 +204,30 @@
                  halo_recv.at[which, c, 1], (line, below)),
         ]
 
+    def ends_copy(which, c, d):
+        return pltpu.make_async_remote_copy(
+            src_ref=ends_out.at[which, cut(c)], dst_ref=ends_in.at[which, d, cut(c)],
+            send_sem=ends_send.at[which, c, d], recv_sem=ends_recv.at[which, c, d],
+            device_id=line_peers[d], device_id_type=MESH,
+        )
+
+    def reaches(which, d):
+        if which:
+            return line + d + 1 >= n_line, line + n_line - d - 1 < n_line
+        return line + d + 1 < n_line, line >= d + 1
+
     def send_ends(which, c):
-        ends[which, c] = [
-            send(ends_out.at[which, cut(c)], ends_in.at[which, d, cut(c)], ends_send.at[which, c, d],
-                 ends_recv.at[which, c, d], peer)
-            for d, peer in enumerate(line_peers)
-        ]
+        for d in range(n_line - 1):
+            @pl.when(reaches(which, d)[0])
+            def _():
+                ends_copy(which, c, d).start()
+
+    def wait_ends(which, c, sent):
+        for d in range(n_line - 1):
+            @pl.when(reaches(which, d)[0 if sent else 1])
+            def _():
+                copy = ends_copy(which, c, d)
+                copy.wait_send() if sent else copy.wait_recv()
 
     for load in loads:
         load.wait()
@@ -249,15 +268,12 @@
         )
 
     def entry(which, c):
-        for copy in ends[which, c]:
-            copy.wait_recv()
+        wait_ends(which, c, False)
         total = jnp.zeros((widths[c], n_point), jnp.float32)
         carried = jnp.ones((1, n_point), jnp.float32)
         for d in range(1, n_line):
             slot = n_line - d - 1 if which else d - 1
-            reached = (line + d < n_line) if which else (line >= d)
-            reached = reached.astype(jnp.float32)
-            total = total + (carried * reached) * ends_in[which, slot, cut(c)]
+            total = total + carried * ends_in[which, slot, cut(c)]
             carried = carried * rates_in[slot, which, 0:1]
         return total
 
@@ -363,33 +379,39 @@
             cross = jnp.dot(top, low[k, :till], preferred_element_type=jnp.float32)
             o_ref[k, cut(c)] = both[:wide] + both[wide:] + cross
 
+    def drain(keep):
+        while len(started) > keep:
+            started.pop(0).wait_send()
+
     for c in range(n_chunk):
         first(c)
-        if c:
-            first_entry(c - 1)
-    first_entry(n_chunk - 1)
+        first_entry(c)
 
     def stage(c, which):
-        if which == 0:
-            second(c)
-            return
-        if which == 1:
-            second_entry(c)
-            sums[c] = panel(c)
-        else:
+        if which:
+            if c == n_chunk - 1:
+                drain(len(flights[c]))
+                if which == 1:
+                    for side in range(2):
+                        for part in range(n_chunk):
+                            wait_ends(side, part, True)
             gram_collect(c)
-        if which <= len(phases):
-            gram_send_phase(c, which - 1)
+        if which < len(phases):
+            gram_send_phase(c, which)
         else:
             factor(c)
 
-    n_stages = len(phases) + 2
-    for now in range(n_chunk + n_stages - 1):
-        for c in range(min(now, n_chunk - 1), -1, -1):
-            if now - c < n_stages:
+    for now in range(n_chunk + len(phases)):
+        if now < n_chunk:
+            second(now)
+        for c in range(min(now, n_chunk)):
+            if now - c <= len(phases):
                 stage(c, now - c)
-    for copy in started:
-        copy.wait_send()
+        if now < n_chunk:
+            second_entry(now)
+            sums[now] = panel(now)
+            stage(now, 0)
+    drain(0)
 
 
 def local(n_line, n_tile, forcing, block_inverse, wall_rates, span_couple):

time: 40.4 us -> 39 us (0.965)
  Pallas kernels: 39.5 us -> 38.2 us
    pallas_call x1, Pallas kernels: 39.5 us -> 38.2 us  [local(): pl.pallas_call(functools.partial(kernel, n_line, n_tile, widths, phases,...]
where the time goes in v6:
time: 39 us; the launch traced here: 38.9 us
  Pallas kernels  38.2 us (98%)
  local copies, waits for them, and re-layouts  0.73 us (2%)
    pallas_call x1, Pallas kernels, local(): pl.pallas_call(functools.partial(kernel, n_line, n_tile, widths, phases,...  38.2 us

profile of v6, /device:TPU:0, one launch (start us, length us, event | category | flops | bytes accessed | tf_op | source)
XLA Modules:
  0.0 38.9 jit_solution(2493250049750528950)
XLA Ops:
  0.0 38.2 %shard_map.46 = f32[10,64,128]{2,1,0:T(8,128)S(1)} custom-call(f32[10,64,128]{2,1,0:T(8,128)} %bitcast.5, f32[10,10,1,128]{3,2,1,0:T(1,128)} %a_in.1, f32[2,10,1,128]{3,2,1,0:T(1,128)} %w_in.1, f32[10]{0:T(128)} %s_in.1), custom_call_target="tpu_custom_call" | custom-call | tf_op jit(solution)/shard_map/pallas_call | solution.py:430
  38.2 0.7 %copy.7 = f32[10,64,1,128]{3,2,1,0:T(1,128)} copy(f32[10,64,1,128]{3,2,1,0:T(1,128)S(1)} %bitcast.4) | data formatting | bytes 655360

commit v7 on v2

--- a/solution.py
+++ b/solution.py
@@ -86,8 +86,8 @@
 
 def kernel(
     n_line, n_tile, n_chunk, phases, scale_value,
-    f_in, a_in, w_in, s_in, o_out,
-    f_ref, a_ref, w_ref, s_ref, o_ref, load_sem, save_sem,
+    f_in, a_in, w_in, s_in, o_ref,
+    f_ref, a_ref, w_ref, s_ref, load_sem,
     start, z_low, z_high, rise, y_low, y_high, fall,
     edge_out, edge_in, ends_out, ends_in, enter, rates_out, rates_in, steps, whole,
     gram_out, gram_in, halo_send, halo_recv, edge_send, edge_recv, ends_send, ends_recv,
@@ -109,6 +109,7 @@
     lower_line = (lax.rem(line + n_line - 1, n_line), tile)
     gram_peers = [[peer_id(ph, step, n_line) for step in phase_peers(ph, n_line)] for ph in phases]
 
+    ends_in[...] = jnp.zeros(ends_in.shape, jnp.float32)
     greet = [(line, above), (line, below)] + [p for peers in gram_peers for p in peers]
     barrier = pltpu.get_barrier_semaphore()
     for peer in greet:
@@ -126,12 +127,10 @@
         return copy
 
     def cut(c):
-        return pl.ds(c * wide, wide)
+        return pl.ds(pl.multiple_of(c * wide, wide), wide)
 
     lane3 = lax.broadcasted_iota(jnp.int32, (n_comp, 1, n_point), 2)
-    lane = lax.broadcasted_iota(jnp.int32, (wide, n_point), 1)
     lane8 = lax.broadcasted_iota(jnp.int32, (ROWS, n_point), 1)
-    lane_big = lax.broadcasted_iota(jnp.int32, (n_comp, wide, n_point), 2)
     strides = scan_strides(n_point)
 
     def turn(value, by):
@@ -153,7 +152,7 @@
 
     def spread(packed):
         return jnp.stack(
-            [jnp.broadcast_to(packed[:, k : k + 1], (wide, n_point)) for k in range(n_comp)], axis=0
+            [jnp.broadcast_to(packed[:, k : k + 1], packed.shape) for k in range(n_comp)], axis=0
         )
 
     def sweep(value, side):
@@ -165,36 +164,66 @@
                 slot += 1
         return value
 
-    halos = {}
-    edges, ends, rates = [], {}, []
-
-    def send_halo(which, c, field, low, high):
-        halos[which, c] = [
-            send(field.at[:, cut(c)], low.at[:, cut(c)], halo_send.at[which, c, 0],
-                 halo_recv.at[which, c, 0], (line, above)),
-            send(field.at[:, cut(c)], high.at[:, cut(c)], halo_send.at[which, c, 1],
-                 halo_recv.at[which, c, 1], (line, below)),
+    rates = []
+
+    def halo_copies(which, c):
+        field, low, high = ((start, z_low, z_high), (rise, y_low, y_high))[which]
+        return [
+            pltpu.make_async_remote_copy(
+                src_ref=field.at[:, cut(c)], dst_ref=there.at[:, cut(c)],
+                send_sem=halo_send.at[which, c, side], recv_sem=halo_recv.at[which, c, side],
+                device_id=(line, to), device_id_type=MESH,
+            )
+            for side, (there, to) in enumerate(((low, above), (high, below)))
         ]
 
+    def edge_copy(c):
+        return pltpu.make_async_remote_copy(
+            src_ref=edge_out.at[cut(c)], dst_ref=edge_in.at[cut(c)], send_sem=edge_send.at[c],
+            recv_sem=edge_recv.at[c], device_id=lower_line, device_id_type=MESH,
+        )
+
+    def ends_copy(which, c, d):
+        return pltpu.make_async_remote_copy(
+            src_ref=ends_out.at[which, cut(c)], dst_ref=ends_in.at[which, d, cut(c)],
+            send_sem=ends_send.at[which, c, d], recv_sem=ends_recv.at[which, c, d],
+            device_id=line_peers[d], device_id_type=MESH,
+        )
+
+    def reaches(which, d):
+        if which:
+            return line + d + 1 >= n_line, line + n_line - d - 1 < n_line
+        return line + d + 1 < n_line, line >= d + 1
+
     def send_ends(which, c):
-        ends[which, c] = [
-            send(ends_out.at[which, cut(c)], ends_in.at[which, d, cut(c)], ends_send.at[which, c, d],
-                 ends_recv.at[which, c, d], peer)
-            for d, peer in enumerate(line_peers)
-        ]
+        for d in range(n_line - 1):
+            @pl.when(reaches(which, d)[0])
+            def _():
+                ends_copy(which, c, d).start()
+
+    def wait_ends(which, c, sent):
+        for d in range(n_line - 1):
+            @pl.when(reaches(which, d)[0 if sent else 1])
+            def _():
+                copy = ends_copy(which, c, d)
+                copy.wait_send() if sent else copy.wait_recv()
 
     for load in loads:
         load.wait()
-    for c in range(n_chunk):
-        field = apply_block(f_ref[:, c * wide : (c + 1) * wide])
+    def begin(c, _):
+        field = apply_block(f_ref[:, cut(c)])
         start[:, cut(c)] = field
         edge_out[cut(c)] = pack(field, 0)
-        if c == 0:
+
+        @pl.when(c == 0)
+        def _():
             pl.semaphore_wait(barrier, len(greet))
-        send_halo(0, c, start, z_low, z_high)
-        edges.append(
-            send(edge_out.at[cut(c)], edge_in.at[cut(c)], edge_send.at[c], edge_recv.at[c], lower_line)
-        )
+
+        for copy in halo_copies(0, c) + [edge_copy(c)]:
+            copy.start()
+        return 0
+
+    lax.fori_loop(0, n_chunk, begin, 0)
 
     for side in range(2):
         rate = w_ref[side]
@@ -216,32 +245,29 @@
         rates.append(send(rates_out, rates_in.at[d], rates_send.at[d], rates_recv.at[d], peer))
 
     def coupled(c, low, high):
-        beside = low[:, c * wide : (c + 1) * wide] + high[:, c * wide : (c + 1) * wide]
+        beside = low[:, cut(c)] + high[:, cut(c)]
         return jnp.stack(
-            [f_ref[k, c * wide : (c + 1) * wide] + s_ref[k] * beside[k] for k in range(n_comp)], axis=0
+            [f_ref[k, cut(c)] + s_ref[k] * beside[k] for k in range(n_comp)], axis=0
         )
 
     def entry(which, c):
-        for copy in ends[which, c]:
-            copy.wait_recv()
+        wait_ends(which, c, False)
         total = jnp.zeros((wide, n_point), jnp.float32)
         carried = jnp.ones((1, n_point), jnp.float32)
         for d in range(1, n_line):
             slot = n_line - d - 1 if which else d - 1
-            reached = (line + d < n_line) if which else (line >= d)
-            reached = reached.astype(jnp.float32)
-            total = total + (carried * reached) * ends_in[which, slot, cut(c)]
+            total = total + carried * ends_in[which, slot, cut(c)]
             carried = carried * rates_in[slot, which, 0:1]
         return total
 
     def first(c):
-        for copy in halos[0, c] + [edges[c]]:
+        for copy in halo_copies(0, c) + [edge_copy(c)]:
             copy.wait_recv()
         source = apply_block(coupled(c, z_low, z_high))
         last = (line < n_line - 1).astype(jnp.float32)
         over = jnp.where(
-            lane_big == n_point - 1, spread(edge_in[cut(c)] * last),
-            turn(start[:, c * wide : (c + 1) * wide], -1),
+            lane3 == n_point - 1, spread(edge_in[cut(c)] * last),
+            turn(start[:, cut(c)], -1),
         )
         value = sweep(source + w_ref[1] * over, 0)
         rise[:, cut(c)] = value
@@ -249,20 +275,23 @@
         send_ends(0, c)
 
     def first_entry(c):
-        if c == 0:
+        @pl.when(c == 0)
+        def _():
             for copy in rates:
                 copy.wait_recv()
+
         total = entry(0, c)
         enter[cut(c)] = total
         rise[:, cut(c)] = rise[:, cut(c)] + whole[0] * spread(total)
-        send_halo(1, c, rise, y_low, y_high)
+        for copy in halo_copies(1, c):
+            copy.start()
 
     def second(c):
-        for copy in halos[1, c]:
+        for copy in halo_copies(1, c):
             copy.wait_recv()
         source = apply_block(coupled(c, y_low, y_high))
         under = jnp.where(
-            lane_big == 0, spread(enter[cut(c)]), turn(rise[:, c * wide : (c + 1) * wide], 1)
+            lane3 == 0, spread(enter[cut(c)]), turn(rise[:, cut(c)], 1)
         )
         value = sweep(source + w_ref[0] * under, 1)
         fall[:, cut(c)] = value
@@ -272,12 +301,29 @@
     def second_entry(c):
         fall[:, cut(c)] = fall[:, cut(c)] + whole[1] * spread(entry(1, c))
 
-    for work, finish in ((first, first_entry), (second, second_entry)):
-        for c in range(n_chunk):
-            work(c)
-            if c:
+    def sweeps(work, finish):
+        def step(c, _):
+            @pl.when(c < n_chunk)
+            def _():
+                work(c)
+
+            @pl.when(c > 0)
+            def _():
                 finish(c - 1)
-        finish(n_chunk - 1)
+
+            return 0
+
+        lax.fori_loop(0, n_chunk + 1, step, 0)
+
+    sweeps(first, first_entry)
+    sweeps(second, second_entry)
+
+    def drain(c, _):
+        for copy in halo_copies(0, c) + halo_copies(1, c) + [edge_copy(c)]:
+            copy.wait_send()
+        for side in range(2):
+            wait_ends(side, c, True)
+        return 0
 
     total = jnp.zeros((2 * n_cols, 2 * n_cols), jnp.float32)
     for k in range(n_comp):
@@ -298,6 +344,10 @@
                 send(gram_out.at[i], gram_in.at[slot], gram_send.at[slot], gram_recv.at[slot], peer)
             )
             slot += 1
+        if i == 0:
+            lax.fori_loop(0, n_chunk, drain, 0)
+            for copy in rates:
+                copy.wait_send()
         for j, copy in enumerate(copies):
             copy.wait_recv()
             packed = packed + gram_in[slot - len(copies) + j]
@@ -305,17 +355,12 @@
 
     high, low = split(eliminate(gram) * scale_value)
     left = jnp.concatenate([high, high, low], axis=1)
-    saves = []
     for k in range(n_comp):
         top, rest = split(fall[k])
         o_ref[k] = jnp.dot(
             left, jnp.concatenate([top, rest, top], axis=0), preferred_element_type=jnp.float32
         )
-        saves.append(pltpu.make_async_copy(o_ref.at[k], o_out.at[k], save_sem.at[k]))
-        saves[k].start()
-    for save in saves:
-        save.wait()
-    for copy in started:
+    for copy in started[len(rates) :]:
         copy.wait_send()
 
 
@@ -330,19 +375,18 @@
     field = pltpu.VMEM((n_comp, n_cols, n_point), jnp.float32)
     dma = pltpu.SemaphoreType.DMA
     f32 = jnp.float32
+    inputs = (forcing.reshape(n_comp, n_cols, n_point), block_inverse, wall_rates, span_couple)
     out = pl.pallas_call(
         functools.partial(kernel, n_line, n_tile, n_chunk, phases, scale_value),
-        out_shape=jax.ShapeDtypeStruct((n_comp, n_cols, n_point), f32),
+        out_shape=pltpu.VMEM((n_comp, n_cols, n_point), f32),
         in_specs=[pl.BlockSpec(memory_space=pltpu.HBM)] * 4,
-        out_specs=pl.BlockSpec(memory_space=pltpu.HBM),
+        out_specs=pl.BlockSpec(memory_space=pltpu.VMEM),
         scratch_shapes=[
             field,
             pltpu.VMEM(block_inverse.shape, f32),
             pltpu.VMEM(wall_rates.shape, f32),
             pltpu.SMEM(span_couple.shape, f32),
-            field,
             dma((4,)),
-            dma((n_comp,)),
         ]
         + [field] * 7
         + [
@@ -369,9 +413,9 @@
             dma((n_gram,)),
         ],
         compiler_params=pltpu.CompilerParams(
-            collective_id=0, has_side_effects=True, vmem_limit_bytes=64 * 1024 * 1024
+            collective_id=0, has_side_effects=True, vmem_limit_bytes=32 * 1024 * 1024
         ),
-    )(forcing.reshape(n_comp, n_cols, n_point), block_inverse, wall_rates, span_couple)
+    )(*[pltpu.with_memory_space_constraint(value, pltpu.HBM) for value in inputs])
     return out.reshape(n_comp, n_cols, 1, n_point)
 
 

time: 39.4 us -> 37.7 us (0.957)
  local copies, waits for them, and re-layouts: 1.72 us -> 0.73 us
  Pallas kernels: 37.5 us -> 36.8 us
    unnamed x1, local copies, waits for them, and re-layouts: 1.72 us -> 0.73 us
    pallas_call x1, Pallas kernels: 37.5 us -> 36.8 us  [local(): pl.pallas_call(functools.partial(kernel, n_line, n_tile, n_chunk, phases,...]
where the time goes in v7:
time: 37.7 us; the launch traced here: 37.5 us
  Pallas kernels  36.8 us (98%)
  local copies, waits for them, and re-layouts  0.73 us (2%)
    pallas_call x1, Pallas kernels, local(): pl.pallas_call(functools.partial(kernel, n_line, n_tile, n_chunk, phases,...  36.8 us

profile of v7, /device:TPU:0, one launch (start us, length us, event | category | flops | bytes accessed | tf_op | source)
XLA Modules:
  0.0 37.5 jit_solution(2920731346031426437)
XLA Ops:
  0.0 36.8 %shard_map.46 = f32[10,64,128]{2,1,0:T(8,128)S(1)} custom-call(f32[10,64,128]{2,1,0:T(8,128)} %bitcast.5, f32[10,10,1,128]{3,2,1,0:T(1,128)} %a_in.1, f32[2,10,1,128]{3,2,1,0:T(1,128)} %w_in.1, f32[10]{0:T(128)} %s_in.1), custom_call_target="tpu_custom_call" | custom-call | tf_op jit(solution)/shard_map/pallas_call | solution.py:379
  36.8 0.7 %copy.7 = f32[10,64,1,128]{3,2,1,0:T(1,128)} copy(f32[10,64,1,128]{3,2,1,0:T(1,128)S(1)} %bitcast.4) | data formatting | bytes 655360

commit v8 on v7

--- a/solution.py
+++ b/solution.py
@@ -368,7 +368,7 @@
     n_comp, n_cols, n_station, n_point = forcing.shape
     assert n_station == 1
     scale_value = math.sqrt(n_comp * n_station * n_tile * n_point * n_line)
-    n_chunk = 4
+    n_chunk = 2
     phases = reduce_phases(n_line, n_tile)
     n_gram = sum(len(phase_peers(ph, n_line)) for ph in phases)
     n_steps = sum(reach - 1 for _, reach in scan_strides(n_point))

time: 37.7 us -> 39.3 us (1.042)
  Pallas kernels: 36.8 us -> 38.4 us
    pallas_call x1, Pallas kernels: 36.8 us -> 38.4 us  [local(): pl.pallas_call(functools.partial(kernel, n_line, n_tile, n_chunk, phases,...]
where the time goes in v8:
time: 39.3 us; the launch traced here: 39.2 us
  Pallas kernels  38.4 us (98%)
  local copies, waits for them, and re-layouts  0.73 us (2%)
    pallas_call x1, Pallas kernels, local(): pl.pallas_call(functools.partial(kernel, n_line, n_tile, n_chunk, phases,...  38.4 us

profile of v8, /device:TPU:0, one launch (start us, length us, event | category | flops | bytes accessed | tf_op | source)
XLA Modules:
  0.0 39.2 jit_solution(2762069184467012060)
XLA Ops:
  0.0 38.4 %shard_map.46 = f32[10,64,128]{2,1,0:T(8,128)S(1)} custom-call(f32[10,64,128]{2,1,0:T(8,128)} %bitcast.5, f32[10,10,1,128]{3,2,1,0:T(1,128)} %a_in.1, f32[2,10,1,128]{3,2,1,0:T(1,128)} %w_in.1, f32[10]{0:T(128)} %s_in.1), custom_call_target="tpu_custom_call" | custom-call | tf_op jit(solution)/shard_map/pallas_call | solution.py:379
  38.5 0.7 %copy.7 = f32[10,64,1,128]{3,2,1,0:T(1,128)} copy(f32[10,64,1,128]{3,2,1,0:T(1,128)S(1)} %bitcast.4) | data formatting | bytes 655360

commit v9 on v7

--- a/solution.py
+++ b/solution.py
@@ -52,6 +52,12 @@
     return high, low
 
 
+def inverse_of(value):
+    guess = pl.reciprocal(value, approx=True)
+    guess = guess * (2.0 - value * guess)
+    return guess * (2.0 - value * guess)
+
+
 def eliminate(gram):
     n = gram.shape[0]
     row = lax.broadcasted_iota(jnp.int32, (n, n), 0)
@@ -60,28 +66,37 @@
     blocks = [both[v * ROWS : (v + 1) * ROWS] for v in range(n // ROWS)]
     shape = (ROWS, 2 * n)
     sub = lax.broadcasted_iota(jnp.int32, shape, 0)
-    scales = []
     for q in range(n // ROWS):
-        live = range(q, n // ROWS)
+        later = range(q + 1, n // ROWS)
         cols = [
-            {v: jnp.broadcast_to(blocks[v][:, ROWS * q + c : ROWS * q + c + 1], shape) for v in live}
+            {
+                v: jnp.broadcast_to(blocks[v][:, ROWS * q + c : ROWS * q + c + 1], shape)
+                for v in range(q, n // ROWS)
+            }
             for c in range(ROWS)
         ]
-        scale = jnp.zeros(shape, jnp.float32)
+        cell = {
+            (i, j): jnp.broadcast_to(cols[j][q][i : i + 1], shape)
+            for i in range(ROWS) for j in range(i + 1)
+        }
+        lines = [jnp.broadcast_to(blocks[q][i : i + 1], shape) for i in range(ROWS)]
         for c in range(ROWS):
-            pivot = jnp.broadcast_to(cols[c][q][c : c + 1], shape)
-            inv = 1.0 / pivot
-            scale = jnp.where(sub == c, lax.rsqrt(pivot), scale)
-            factor = {v: cols[c][v] * inv for v in live}
-            factor[q] = jnp.where(sub > c, factor[q], 0.0)
-            top = jnp.broadcast_to(blocks[q][c : c + 1], shape)
-            tops = [jnp.broadcast_to(cols[e][q][c : c + 1], shape) for e in range(c + 1, ROWS)]
-            for v in live:
-                blocks[v] = blocks[v] - factor[v] * top
+            inv = inverse_of(cell[c, c])
+            for i in range(c + 1, ROWS):
+                share = cell[i, c] * inv
+                for j in range(c + 1, i + 1):
+                    cell[i, j] = cell[i, j] - share * cell[j, c]
+                lines[i] = lines[i] - share * lines[c]
+            for v in later:
+                share = cols[c][v] * inv
+                blocks[v] = blocks[v] - share * lines[c]
                 for e in range(c + 1, ROWS):
-                    cols[e][v] = cols[e][v] - factor[v] * tops[e - c - 1]
-        scales.append(scale)
-    return jnp.concatenate([b * s for b, s in zip(blocks, scales)], axis=0)[:, n:]
+                    cols[e][v] = cols[e][v] - share * cell[e, c]
+        done = lines[0] * lax.rsqrt(cell[0, 0])
+        for i in range(1, ROWS):
+            done = jnp.where(sub == i, lines[i] * lax.rsqrt(cell[i, i]), done)
+        blocks[q] = done
+    return jnp.concatenate(blocks, axis=0)[:, n:]
 
 
 def kernel(

time: 37.7 us -> 38.3 us (1.016)
  Pallas kernels: 36.8 us -> 37.4 us
    pallas_call x1, Pallas kernels: 36.8 us -> 37.4 us  [local(): pl.pallas_call(functools.partial(kernel, n_line, n_tile, n_chunk, phases,...]
where the time goes in v9:
time: 38.3 us; the launch traced here: 38.1 us
  Pallas kernels  37.4 us (98%)
  local copies, waits for them, and re-layouts  0.73 us (2%)
    pallas_call x1, Pallas kernels, local(): pl.pallas_call(functools.partial(kernel, n_line, n_tile, n_chunk, phases,...  37.4 us

profile of v9, /device:TPU:0, one launch (start us, length us, event | category | flops | bytes accessed | tf_op | source)
XLA Modules:
  0.0 38.1 jit_solution(14728568728230489678)
XLA Ops:
  0.0 37.4 %shard_map.46 = f32[10,64,128]{2,1,0:T(8,128)S(1)} custom-call(f32[10,64,128]{2,1,0:T(8,128)} %bitcast.5, f32[10,10,1,128]{3,2,1,0:T(1,128)} %a_in.1, f32[2,10,1,128]{3,2,1,0:T(1,128)} %w_in.1, f32[10]{0:T(128)} %s_in.1), custom_call_target="tpu_custom_call" | custom-call | tf_op jit(solution)/shard_map/pallas_call | solution.py:394
  37.4 0.7 %copy.7 = f32[10,64,1,128]{3,2,1,0:T(1,128)} copy(f32[10,64,1,128]{3,2,1,0:T(1,128)S(1)} %bitcast.4) | data formatting | bytes 655360

commit v10 on v8

--- a/solution.py
+++ b/solution.py
@@ -368,7 +368,7 @@
     n_comp, n_cols, n_station, n_point = forcing.shape
     assert n_station == 1
     scale_value = math.sqrt(n_comp * n_station * n_tile * n_point * n_line)
-    n_chunk = 2
+    n_chunk = 8
     phases = reduce_phases(n_line, n_tile)
     n_gram = sum(len(phase_peers(ph, n_line)) for ph in phases)
     n_steps = sum(reach - 1 for _, reach in scan_strides(n_point))

time: 39.3 us -> 42.7 us (1.087)
  Pallas kernels: 38.4 us -> 41.7 us
    pallas_call x1, Pallas kernels: 38.4 us -> 41.7 us  [local(): pl.pallas_call(functools.partial(kernel, n_line, n_tile, n_chunk, phases,...]
where the time goes in v10:
time: 42.7 us; the launch traced here: 42.4 us
  Pallas kernels  41.7 us (98%)
  local copies, waits for them, and re-layouts  0.73 us (2%)
    pallas_call x1, Pallas kernels, local(): pl.pallas_call(functools.partial(kernel, n_line, n_tile, n_chunk, phases,...  41.7 us

profile of v10, /device:TPU:0, one launch (start us, length us, event | category | flops | bytes accessed | tf_op | source)
XLA Modules:
  0.0 42.4 jit_solution(13341438320012408839)
XLA Ops:
  0.0 41.7 %shard_map.46 = f32[10,64,128]{2,1,0:T(8,128)S(1)} custom-call(f32[10,64,128]{2,1,0:T(8,128)} %bitcast.5, f32[10,10,1,128]{3,2,1,0:T(1,128)} %a_in.1, f32[2,10,1,128]{3,2,1,0:T(1,128)} %w_in.1, f32[10]{0:T(128)} %s_in.1), custom_call_target="tpu_custom_call" | custom-call | tf_op jit(solution)/shard_map/pallas_call | solution.py:379
  41.7 0.7 %copy.7 = f32[10,64,1,128]{3,2,1,0:T(1,128)} copy(f32[10,64,1,128]{3,2,1,0:T(1,128)S(1)} %bitcast.4) | data formatting | bytes 655360
